TPU v7x, 512 devices: a whole 4x4x16 slice. The times are simulated.
512 devices in a mesh: gauss: 128 (over z, x, core), view: 4 (over y).
Axes of the slice: x: 4, y: 4, z: 16, core: 2. Of those that a mesh axis runs over, the one named last changes fastest.
Arguments:
- params: float32 [59, 65536], P(None, 'gauss'), as said below
- first_moment: float32 [59, 65536], P(None, 'gauss'), may hold values from -0.6 to 0.6
- second_moment: float32 [59, 65536], P(None, 'gauss'), may hold values from 0.0001 to 0.01
- cameras: float32 [4, 12], P('view'), as said below
- send_rows: int32 [4, 128, 512], P('view', 'gauss'), may hold values from 0 to 511, as said below
- lists: int32 [4, 256, 256], P('view', 'gauss'), may hold values from 0 to 511, as said below
- counts: int32 [4, 256], P('view', 'gauss'), may hold values from 1 to 256, 32768 in all within a row
- tile_ids: int32 [4, 256], P('view', 'gauss'), may hold values from 0 to 8159, as said below
- target: float32 [4, 256, 3, 256], P('view', 'gauss'), may hold values from 0 to 1
Outputs:
- new_params: float32 [59, 65536], P(None, 'gauss')
- new_first: float32 [59, 65536], P(None, 'gauss')
- new_second: float32 [59, 65536], P(None, 'gauss')
- tile_loss: float32 [4, 256], P('view', 'gauss')
Inputs may be any that keep to these rules, and one draw needn't show every extreme that they name: `send_rows`: for each view and sender the 512 entries name every local row once. The 4 rows that a sender sends to one renderer form a group that goes whole to one renderer in every view, possibly another one in each view. `lists`: each tile's list names distinct slots; entries at positions counts or later are ignored. `tile_ids`: tiles of one view are distinct. Each view's counts sum to 32768. `params`: rows 0 and 1 lie within 7.5, row 2 within 0.25; rows 3 to 5 in [-4.5, -2]; row 6 in [0.5, 1.5], rows 7 to 9 within 1; row 10 in [-5.5, -1.5]. `cameras`: the matrix lies within 0.01 of the identity entrywise; translations x and y within 0.3, z in [7.95, 8.05].
All inputs are finite; a program needn't handle non-finite values. No bound on the sum of `counts` on one device may be relied on, other than what follows from the above.
Results may differ from a plain program's by a relative error of at most 0.0003.
Values sent between devices are 32-bit elements; how exact they have to be, the bound alone decides.
A program may use at most 64 MiB of HBM per device.

v0:
```python
import jax
import jax.numpy as jnp
from jax import lax
from jax.sharding import PartitionSpec as P

focal_length = 1100.0
centre_x = 960.0
centre_y = 540.0
beta_one = 0.9
beta_two = 0.999
adam_eps = 1e-15
adam_step = 100.0
sh_zero = 0.28209479177387814
sh_one = 0.4886025119029199
sh_two = [
    1.0925484305920792,
    -1.0925484305920792,
    0.31539156525252005,
    -1.0925484305920792,
    0.5462742152960396,
]
sh_three = [
    -0.5900435899266435,
    2.890611442640554,
    -0.4570457994644658,
    0.3731763325901154,
    -0.4570457994644658,
    1.445305721320277,
    -0.5900435899266435,
]


def harmonics(dir_x, dir_y, dir_z):
    sq_x = dir_x * dir_x
    sq_y = dir_y * dir_y
    sq_z = dir_z * dir_z
    return [
        sh_zero + 0.0 * dir_x,
        -sh_one * dir_y,
        sh_one * dir_z,
        -sh_one * dir_x,
        sh_two[0] * dir_x * dir_y,
        sh_two[1] * dir_y * dir_z,
        sh_two[2] * (2.0 * sq_z - sq_x - sq_y),
        sh_two[3] * dir_x * dir_z,
        sh_two[4] * (sq_x - sq_y),
        sh_three[0] * dir_y * (3.0 * sq_x - sq_y),
        sh_three[1] * dir_x * dir_y * dir_z,
        sh_three[2] * dir_y * (4.0 * sq_z - sq_x - sq_y),
        sh_three[3] * dir_z * (2.0 * sq_z - 3.0 * sq_x - 3.0 * sq_y),
        sh_three[4] * dir_x * (4.0 * sq_z - sq_x - sq_y),
        sh_three[5] * dir_z * (sq_x - sq_y),
        sh_three[6] * dir_x * (sq_x - 3.0 * sq_y),
    ]


def project(columns, camera):
    mean_x, mean_y, mean_z = (columns[0], columns[1], columns[2])
    scales = jnp.exp(columns[3:6])
    quat_w, quat_x, quat_y, quat_z = (columns[6], columns[7], columns[8], columns[9])
    length = jnp.sqrt(quat_w * quat_w + quat_x * quat_x + quat_y * quat_y + quat_z * quat_z)
    quat_w, quat_x, quat_y, quat_z = (
        quat_w / length,
        quat_x / length,
        quat_y / length,
        quat_z / length,
    )
    turn = [
        [
            1.0 - 2.0 * (quat_y * quat_y + quat_z * quat_z),
            2.0 * (quat_x * quat_y - quat_w * quat_z),
            2.0 * (quat_x * quat_z + quat_w * quat_y),
        ],
        [
            2.0 * (quat_x * quat_y + quat_w * quat_z),
            1.0 - 2.0 * (quat_x * quat_x + quat_z * quat_z),
            2.0 * (quat_y * quat_z - quat_w * quat_x),
        ],
        [
            2.0 * (quat_x * quat_z - quat_w * quat_y),
            2.0 * (quat_y * quat_z + quat_w * quat_x),
            1.0 - 2.0 * (quat_x * quat_x + quat_y * quat_y),
        ],
    ]
    world = [[turn[outer][inner] * scales[inner] for inner in range(3)] for outer in range(3)]
    posed = [
        camera[3 * outer] * mean_x
        + camera[3 * outer + 1] * mean_y
        + camera[3 * outer + 2] * mean_z
        + camera[9 + outer]
        for outer in range(3)
    ]
    cam_x, cam_y, depth = posed
    framed = [
        [
            camera[3 * outer] * world[0][inner]
            + camera[3 * outer + 1] * world[1][inner]
            + camera[3 * outer + 2] * world[2][inner]
            for inner in range(3)
        ]
        for outer in range(3)
    ]
    inverse = 1.0 / depth
    row_top = [
        focal_length * inverse * (framed[0][inner] - cam_x * inverse * framed[2][inner])
        for inner in range(3)
    ]
    row_low = [
        focal_length * inverse * (framed[1][inner] - cam_y * inverse * framed[2][inner])
        for inner in range(3)
    ]
    cov_a = row_top[0] * row_top[0] + row_top[1] * row_top[1] + row_top[2] * row_top[2] + 0.3
    cov_b = row_top[0] * row_low[0] + row_top[1] * row_low[1] + row_top[2] * row_low[2]
    cov_c = row_low[0] * row_low[0] + row_low[1] * row_low[1] + row_low[2] * row_low[2] + 0.3
    determinant = cov_a * cov_c - cov_b * cov_b
    centre_u = focal_length * cam_x * inverse + centre_x
    centre_v = focal_length * cam_y * inverse + centre_y
    distance = jnp.sqrt(cam_x * cam_x + cam_y * cam_y + depth * depth)
    basis = harmonics(cam_x / distance, cam_y / distance, depth / distance)
    colours = []
    for channel in range(3):
        total = 0.5 + 0.0 * mean_x
        for order in range(16):
            total = total + basis[order] * columns[11 + 3 * order + channel]
        colours.append(total)
    opacity = jax.nn.sigmoid(columns[10])
    return jnp.stack(
        [
            centre_u,
            centre_v,
            cov_c / determinant,
            -cov_b / determinant,
            cov_a / determinant,
            opacity,
            colours[0],
            colours[1],
            colours[2],
        ]
    )


def shade_block(carry, picked, alive, pixel_x, pixel_y):
    transmit, colour = carry
    offset_x = pixel_x[:, None] - picked[0][None, :]
    offset_y = pixel_y[:, None] - picked[1][None, :]
    exponent = (
        -0.5 * (picked[2][None, :] * offset_x * offset_x + picked[4][None, :] * offset_y * offset_y)
        - picked[3][None, :] * offset_x * offset_y
    )
    opacity_map = (picked[5] * alive)[None, :] * jnp.exp(exponent)
    keep_log = jnp.log1p(-opacity_map)
    running = jnp.cumsum(keep_log, axis=1)
    weight = transmit[:, None] * jnp.exp(running - keep_log) * opacity_map
    colour = colour + jnp.dot(weight, picked[6:9].T, precision=lax.Precision.HIGHEST)
    transmit = transmit * jnp.exp(running[:, -1])
    return (transmit, colour)


def render_tile(attributes, entries, count, tile_id, target_tile):
    pixel = jnp.arange(256, dtype=jnp.int32)
    pixel_x = (tile_id % 120 * 16 + pixel % 16).astype(jnp.float32)
    pixel_y = (tile_id // 120 * 16 + pixel // 16).astype(jnp.float32)
    blocks = entries.shape[0] // 256
    picked = jnp.take(attributes, entries, axis=1).reshape(9, blocks, 256).transpose(1, 0, 2)
    alive = (
        (jnp.arange(entries.shape[0], dtype=jnp.int32) < count)
        .astype(jnp.float32)
        .reshape(blocks, 256)
    )
    block_start = jnp.arange(blocks, dtype=jnp.int32) * 256
    shade = jax.checkpoint(shade_block)

    def advance(carry, block):

        def active(state):
            return shade(state, block[0], block[1], pixel_x, pixel_y)

        def passed(state):
            return state

        return (lax.cond(block[2] < count, active, passed, carry), None)

    start = (jnp.ones((256,), jnp.float32), jnp.zeros((256, 3), jnp.float32))
    (transmit, colour), unused = lax.scan(advance, start, (picked, alive, block_start))
    difference = colour.T - target_tile
    return 0.5 * jnp.sum(difference * difference)


def adam(params, first_moment, second_moment, grads):
    rates = jnp.concatenate(
        [
            jnp.full((3,), 0.00016),
            jnp.full((3,), 0.005),
            jnp.full((4,), 0.001),
            jnp.full((1,), 0.05),
            jnp.full((3,), 0.0025),
            jnp.full((45,), 0.000125),
        ]
    ).astype(params.dtype)
    new_first = beta_one * first_moment + (1.0 - beta_one) * grads
    new_second = beta_two * second_moment + (1.0 - beta_two) * grads * grads
    step_size = rates[:, None] / (1.0 - beta_one**adam_step)
    new_params = params - step_size * new_first / (
        jnp.sqrt(new_second / (1.0 - beta_two**adam_step)) + adam_eps
    )
    return (new_params, new_first, new_second)


def body(params, first_moment, second_moment, cameras, send_rows, lists, counts, tile_ids, target):
    camera = cameras[0]
    outgoing = send_rows[0, 0]

    def shade_device(attributes):

        def one_tile(tile_item):
            return render_tile(attributes, tile_item[0], tile_item[1], tile_item[2], tile_item[3])

        return lax.map(one_tile, (lists[0], counts[0], tile_ids[0], target[0]))

    def view_project(columns):
        return project(columns, camera)

    picked = jnp.take(params, outgoing, axis=1)
    received = lax.all_to_all(picked, "gauss", split_axis=1, concat_axis=1, tiled=True)
    attributes, project_back = jax.vjp(view_project, received)
    tile_loss, render_back = jax.vjp(shade_device, attributes)
    attr_grad = render_back(jnp.ones_like(tile_loss))[0]
    slot_grad = project_back(attr_grad)[0]
    returned = lax.all_to_all(slot_grad, "gauss", split_axis=1, concat_axis=1, tiled=True)
    grads = jnp.zeros_like(params).at[:, outgoing].add(returned)
    total = lax.psum(grads, "view")
    new_params, new_first, new_second = adam(params, first_moment, second_moment, total)
    return (new_params, new_first, new_second, tile_loss.reshape(1, -1))


def solution(mesh):
    in_specs = (
        P(None, "gauss"),
        P(None, "gauss"),
        P(None, "gauss"),
        P("view", None),
        P("view", "gauss", None),
        P("view", "gauss", None),
        P("view", "gauss"),
        P("view", "gauss"),
        P("view", "gauss", None, None),
    )
    out_specs = (P(None, "gauss"), P(None, "gauss"), P(None, "gauss"), P("view", "gauss"))
    return jax.shard_map(body, mesh=mesh, in_specs=in_specs, out_specs=out_specs, check_vma=False)
```

profile of v0, /device:TPU:6, one launch (start us, length us, event | category | flops | bytes accessed | tf_op | source)
XLA Modules:
  0.0 241.9 jit_solution(12728218538648837767)
XLA Ops:
  7.2 0.7 compare_select_fusion.4
  8.4 1.3 reduce.130
  10.1 1.0 gather_fusion.1
  11.3 1.0 reshape.3352
  12.3 19.4 %all-to-all-start = ((f32[128,1,236]{2,1,0:T(1,128)}), f32[128,1,236]{2,1,0:T(1,128)S(1)}, u32[]{:S(2)}, u32[]{:S(2)}) async-start(f32[128,1,236]{2,1,0:T(1,128)} %reshape.3352), calls=%async_computation | async-start | bytes 262144 | tf_op jit(solution)/shard_map/all_to_all | solution.py:224
  32.7 0.7 fusion.168
  33.4 14.3 %all-to-all-done = f32[128,1,236]{2,1,0:T(1,128)S(1)} async-done(((f32[128,1,236]{2,1,0:T(1,128)}), f32[128,1,236]{2,1,0:T(1,128)S(1)}, u32[]{:S(2)}, u32[]{:S(2)}) %all-to-all-start) | async-done | bytes 120864 | tf_op jit(solution)/shard_map/all_to_all | solution.py:224
  48.3 0.9 reduce.131
  49.7 5.9 %slice_reduce_fusion.20 = (f32[128,4]{1,0:T(8,128)}, f32[128,4]{1,0:T(8,128)}, f32[128,4]{1,0:T(8,128)}, f32[128,4]{1,0:T(8,128)}, f32[128,4]{1,0:T(8,128)}, /*i...) fusion(f32[59,128,4]{0,2,1:T(4,128)S(1)} %bitcast.179), kind=kLoop, calls=%fused_computation.184 | loop fusion | bytes 77824 | tf_op jit(solution)/shard_map/jvp()/slice | solution.py:124
  55.6 5.8 %slice_reduce_fusion.6 = (f32[128,4]{1,0:T(8,128)}, f32[128,4]{1,0:T(8,128)}, f32[128,4]{1,0:T(8,128)}, f32[128,4]{1,0:T(8,128)}, f32[128,4]{1,0:T(8,128)}, /*in...) fusion(f32[59,128,4]{0,2,1:T(4,128)S(1)} %bitcast.180), kind=kLoop, calls=%fused_computation.170 | loop fusion | bytes 77824 | tf_op jit(solution)/shard_map/jvp()/slice | solution.py:124
  61.4 4.9 %fusion.167 = (f32[1,128,4]{0,2,1:T(4,128)S(1)}, f32[1,128,4]{0,2,1:T(4,128)S(1)}, f32[1,128,4]{0,2,1:T(4,128)S(1)}, f32[128,4]{1,0:T(8,128)S(1)}, f32[128,4]{1,...) fusion(f32[59,128,4]{0,2,1:T(4,128)S(1)} %bitcast.181), kind=kLoop, calls=%fused_computation.479 | loop fusion | bytes 73728 | tf_op jit(solution)/shard_map/jvp()/slice | solution.py:126
  66.3 0.8 slice_reduce_fusion.56
  67.0 0.7 copy.213
  81.9 7.6 %add_add_fusion.21 = (f32[1,128,4]{1,2,0:T(4,128)S(1)}, f32[1,128,4]{1,2,0:T(4,128)S(1)}, f32[1,128,4]{1,2,0:T(4,128)S(1)}, f32[1,128,4]{1,2,0:T(4,128)S(1)}) fusion(f32[1,128,4]{1,2,0:T(4,128)S(1)} %copy.218, f32[1,128,4]{1,2,0:T(4,128)S(1)} %copy.217, f32[1,128,4]{1,2,0:T(4,128)S(1)} %copy.216, f32[]{:T(128)} %bitcast.64, f32[]{:T(128)} %bitcast.63, ...), kind=kLoop, calls=%fused_computation.379 | loop fusion | flops 10240 | bytes 14384 | tf_op jit(solution)/shard_map/jvp()/add | solution.py:87
  90.7 5.8 %fusion.159 = (f32[1,512]{1,0:T(1,128)S(1)}, f32[1,512]{1,0:T(1,128)S(1)}, f32[1,512]{1,0:T(1,128)S(1)}, f32[1,512]{1,0:T(1,128)S(1)}, f32[1,512]{1,0:T(1,128)S(...) fusion(f32[1,512]{1,0:T(1,128)S(1)} %slice.605, ...), kind=kLoop, calls=%fused_computation.477 | loop fusion | flops 65024 | bytes 86052 | tf_op jit(solution)/shard_map/jvp()/div | solution.py:133
  97.9 20.3 %while.67 = (s32[]{:T(128)}, f32[2]{0:T(128)S(1)}, s32[2,256,1]{1,2,0:T(1,128)S(1)}, s32[2,1]{0,1:T(1,128)S(1)}, f32[2,1,256]{2,1,0:T(1,128)S(1)}, /*index=5*/f3...) while((s32[]{:T(128)}, f32[2]{0:T(128)S(1)}, ...), condition=%wide.region_6.7_spmd.clone, body=%wide.region_0.6_spmd.clone.sunk | while | flops 12601618 | bytes 2342214 | solution.py:218
  102.0 0.7 compare_convert_fusion.2
  102.7 4.0 %conditional.6 = (f32[256,3]{0,1:T(4,128)S(1)}, f32[1,1,256]{2,1,0:T(1,128)S(1)}, f32[1,1,9,256]{2,3,1,0:T(8,128)S(1)}, f32[1,1,256]{2,1,0:T(1,128)S(1)}, f32[1,...) conditional(s32[]{:T(128)} %convert_element_type.47, f32[256,3]{0,1:T(4,128)S(1)} %broadcast_in_dim.320, ...), branch_computations={%region_1.1_spmd, %region_2.4_spmd} | conditional | flops 12592640 | bytes 2254648 | solution.py:181
  102.7 0.7 gather_fusion
  104.9 0.9 fusion.63
  112.1 0.7 compare_convert_fusion.2
  112.8 4.0 %conditional.6 = (f32[256,3]{0,1:T(4,128)S(1)}, f32[1,1,256]{2,1,0:T(1,128)S(1)}, f32[1,1,9,256]{2,3,1,0:T(8,128)S(1)}, f32[1,1,256]{2,1,0:T(1,128)S(1)}, f32[1,...) conditional(s32[]{:T(128)} %convert_element_type.47, f32[256,3]{0,1:T(4,128)S(1)} %broadcast_in_dim.320, ...), branch_computations={%region_1.1_spmd, %region_2.4_spmd} | conditional | flops 12592640 | bytes 2254648 | solution.py:181
  112.8 0.7 gather_fusion
  114.9 0.9 fusion.63
  118.8 20.8 %while.66 = (s32[]{:T(128)}, f32[9,512]{0,1:T(8,128)S(1)}, s32[2,256,1]{1,2,0:T(1,128)S(1)}, s32[2,1]{0,1:T(1,128)S(1)}, f32[2,3,256]{2,1,0:T(4,128)S(1)}, /*ind...) while((s32[]{:T(128)}, f32[9,512]{0,1:T(8,128)S(1)}, ...), condition=%wide.region_21.22_spmd, body=%wide.region_7.21_spmd.sunk | while | flops 28723972 | bytes 6037733 | solution.py:218
  118.9 0.7 constant_dynamic-slice_fusion.11
  119.5 7.4 %conditional.5 = (f32[9,256]{1,0:T(8,128)S(1)}) conditional(s32[]{:T(128)} %bitcast.164, () %tuple.442, (f32[2,1,256]{2,1,0:T(1,128)S(1)}, s32[]{:T(128)}, f32[2,1,9,256]{3,2,1,0:T(8,128)S(1)}, f32[2,1,256]{2,1,0:T(1,128)S(1)}, f32[2,1,256]{2,1,0:T(1,128)S(1)}, /*index=5*/f32[2,1,256]{2,1,0:T(1,128)S(1)}, f32[256,3]{0,1:T(4,128)S(1)}) %tuple.443), branch_computations={%region_8.8_spmd, %region_9.19_spmd} | conditional | flops 28720128 | bytes 5982240 | solution.py:181
  121.0 0.9 fusion.22
  122.6 0.7 pad_add_fusion
  123.3 2.3 fusion.34
  127.1 2.0 scatter_fusion
  129.1 0.7 constant_dynamic-slice_fusion.11
  129.8 7.4 %conditional.5 = (f32[9,256]{1,0:T(8,128)S(1)}) conditional(s32[]{:T(128)} %bitcast.164, () %tuple.442, (f32[2,1,256]{2,1,0:T(1,128)S(1)}, s32[]{:T(128)}, f32[2,1,9,256]{3,2,1,0:T(8,128)S(1)}, f32[2,1,256]{2,1,0:T(1,128)S(1)}, f32[2,1,256]{2,1,0:T(1,128)S(1)}, /*index=5*/f32[2,1,256]{2,1,0:T(1,128)S(1)}, f32[256,3]{0,1:T(4,128)S(1)}) %tuple.443), branch_computations={%region_8.8_spmd, %region_9.19_spmd} | conditional | flops 28720128 | bytes 5982240 | solution.py:181
  131.3 0.9 fusion.22
  132.9 0.7 pad_add_fusion
  133.6 2.3 fusion.34
  137.4 2.0 scatter_fusion
  141.6 5.8 %add_add_fusion.12 = (f32[1,512]{1,0:T(1,128)S(1)}, f32[1,512]{1,0:T(1,128)S(1)}, f32[1,512]{1,0:T(1,128)S(1)}, f32[1,512]{1,0:T(1,128)S(1)}, f32[1,512]{1,0:T(1...) fusion(f32[1,512]{1,0:T(1,128)S(1)} %copy-done.35, ...), kind=kLoop, calls=%fused_computation.252 | loop fusion | flops 64512 | bytes 90148 | tf_op jit(solution)/shard_map/transpose(jvp())/add_any | solution.py:70
  147.5 2.0 add_add_fusion.9
  149.6 2.0 multiply_add_fusion.8
  151.6 3.8 %multiply_add_fusion.7 = (f32[1,512]{1,0:T(1,128)S(1)}, f32[1,512]{1,0:T(1,128)S(1)}) fusion(f32[1,512]{1,0:T(1,128)S(1)} %get-tuple-element.1235, f32[1,512]{1,0:T(1,128)S(1)} %get-tuple-element.1234, f32[1,512]{1,0:T(1,128)S(1)} %get-tuple-element.1233, f32[]{:T(128)} %bitcast.54, f32[]{:T(128)} %bitcast.58, f32[]{:T(128)} %bitcast.62, f32[]{:T(128)} %bitcast.51, ...), kind=kLoop, calls=%fused_computation.282 | loop fusion | flops 7168 | bytes 16408 | tf_op jit(solution)/shard_map/transpose(jvp())/add_any | solution.py:88
  155.4 0.7 copy-done.29
  156.8 23.0 %all_to_all.18 = f32[128,1,236]{2,1,0:T(1,128)S(1)} all-to-all(f32[128,1,236]{2,1,0:T(1,128)S(1)} %reshape.3354), channel_id=1, replica_groups=mesh['gauss'=128,'view'=4] {'gauss'}, dimensions={0} | all-to-all | bytes 241664 | tf_op jit(solution)/shard_map/all_to_all | solution.py:229
  179.8 0.9 reduce.132
  180.9 2.4 %scatter_custom_fusion.1 = f32[59,512]{0,1:T(8,128)S(1)} fusion(s32[512]{0:T(512)} %bitcast.265, f32[512,59]{1,0:T(8,128)S(1)} %bitcast.234, f32[]{:T(128)} %constant.373.clone.1), kind=kCustom, calls=%fused_computation.233 | custom fusion | flops 30208 | bytes 121344 | tf_op jit(solution)/shard_map/scatter-add | solution.py:230
  183.3 0.8 copy.212
  184.1 49.0 %all-reduce.76.cloned.1.call-done = f32[59,512]{1,0:T(8,128)} async-done(((f32[59,512]{1,0:T(8,128)}), f32[59,512]{1,0:T(8,128)}) %all-reduce.76.cloned.1.call-update) | async-done | bytes 120848 | tf_op jit(solution)/shard_map/psum | solution.py:231
  233.1 1.7 divide_subtract_fusion
  (465 shorter events, 36.5 us)
Async XLA Ops:
  7.2 2.8 %copy-start = (f32[59,512]{1,0:T(8,128)S(1)}, f32[59,512]{1,0:T(8,128)}, u32[]{:S(2)}) copy-start(f32[59,512]{1,0:T(8,128)} %param.17) | copy-start | bytes 362500
  7.9 1.9 copy-start.92
  12.3 35.5 %all-to-all-start = ((f32[128,1,236]{2,1,0:T(1,128)}), f32[128,1,236]{2,1,0:T(1,128)S(1)}, u32[]{:S(2)}, u32[]{:S(2)}) async-start(f32[128,1,236]{2,1,0:T(1,128)} %reshape.3352), calls=%async_computation | async-start | bytes 262144 | tf_op jit(solution)/shard_map/all_to_all | solution.py:224
  31.7 201.4 %all-reduce.76.cloned.1.call-start = ((), (), s32[]{:S(2)}) async-start(), calls=%async_computation.2 | async-start | bytes 262144 | tf_op jit(solution)/shard_map/psum | solution.py:231
  67.9 22.8 %copy-start.30 = (f32[1,512]{1,0:T(1,128)}, f32[1,512]{1,0:T(1,128)S(1)}, u32[]{:S(2)}) copy-start(f32[1,512]{1,0:T(1,128)S(1)} %slice.605) | copy-start | bytes 6148
  68.0 22.7 %copy-start.32 = (f32[1,512]{1,0:T(1,128)}, f32[1,512]{1,0:T(1,128)S(1)}, u32[]{:S(2)}) copy-start(f32[1,512]{1,0:T(1,128)S(1)} %slice.609) | copy-start | bytes 6148
  68.0 0.8 copy-start.23
  68.1 22.6 %copy-start.34 = (f32[1,512]{1,0:T(1,128)}, f32[1,512]{1,0:T(1,128)S(1)}, u32[]{:S(2)}) copy-start(f32[1,512]{1,0:T(1,128)S(1)} %slice.607) | copy-start | bytes 6148
  68.7 0.8 copy-start.22
  68.8 27.7 %copy-start.36 = (f32[1,512]{1,0:T(1,128)}, f32[1,512]{1,0:T(1,128)S(1)}, u32[]{:S(2)}) copy-start(f32[1,512]{1,0:T(1,128)S(1)} %slice.678) | copy-start | bytes 6148
  68.8 0.8 copy-start.21
  69.0 27.6 %copy-start.38 = (f32[1,512]{1,0:T(1,128)}, f32[1,512]{1,0:T(1,128)S(1)}, u32[]{:S(2)}) copy-start(f32[1,512]{1,0:T(1,128)S(1)} %slice.700) | copy-start | bytes 6148
  69.6 0.8 copy-start.20
  69.7 26.9 %copy-start.40 = (f32[1,512]{1,0:T(1,128)}, f32[1,512]{1,0:T(1,128)S(1)}, u32[]{:S(2)}) copy-start(f32[1,512]{1,0:T(1,128)S(1)} %slice.698) | copy-start | bytes 6148
  69.7 0.8 copy-start.19
  69.8 26.7 %copy-start.42 = (f32[1,512]{1,0:T(1,128)}, f32[1,512]{1,0:T(1,128)S(1)}, u32[]{:S(2)}) copy-start(f32[1,512]{1,0:T(1,128)S(1)} %slice.696) | copy-start | bytes 6148
  70.4 0.8 copy-start.18
  70.5 26.0 %copy-start.44 = (f32[1,512]{1,0:T(1,128)}, f32[1,512]{1,0:T(1,128)S(1)}, u32[]{:S(2)}) copy-start(f32[1,512]{1,0:T(1,128)S(1)} %slice.694) | copy-start | bytes 6148
  70.5 0.8 copy-start.17
  70.6 25.9 %copy-start.46 = (f32[1,512]{1,0:T(1,128)}, f32[1,512]{1,0:T(1,128)S(1)}, u32[]{:S(2)}) copy-start(f32[1,512]{1,0:T(1,128)S(1)} %slice.692) | copy-start | bytes 6148
  71.4 25.2 %copy-start.48 = (f32[1,512]{1,0:T(1,128)}, f32[1,512]{1,0:T(1,128)S(1)}, u32[]{:S(2)}) copy-start(f32[1,512]{1,0:T(1,128)S(1)} %slice.690) | copy-start | bytes 6148
  71.4 0.8 copy-start.15
  71.5 25.1 %copy-start.50 = (f32[1,512]{1,0:T(1,128)}, f32[1,512]{1,0:T(1,128)S(1)}, u32[]{:S(2)}) copy-start(f32[1,512]{1,0:T(1,128)S(1)} %slice.688) | copy-start | bytes 6148
  72.2 24.4 %copy-start.52 = (f32[1,512]{1,0:T(1,128)}, f32[1,512]{1,0:T(1,128)S(1)}, u32[]{:S(2)}) copy-start(f32[1,512]{1,0:T(1,128)S(1)} %slice.686) | copy-start | bytes 6148
  72.3 24.3 %copy-start.54 = (f32[1,512]{1,0:T(1,128)}, f32[1,512]{1,0:T(1,128)S(1)}, u32[]{:S(2)}) copy-start(f32[1,512]{1,0:T(1,128)S(1)} %slice.684) | copy-start | bytes 6148
  73.1 23.6 %copy-start.56 = (f32[1,512]{1,0:T(1,128)}, f32[1,512]{1,0:T(1,128)S(1)}, u32[]{:S(2)}) copy-start(f32[1,512]{1,0:T(1,128)S(1)} %slice.682) | copy-start | bytes 6148
  73.2 23.4 %copy-start.58 = (f32[1,512]{1,0:T(1,128)}, f32[1,512]{1,0:T(1,128)S(1)}, u32[]{:S(2)}) copy-start(f32[1,512]{1,0:T(1,128)S(1)} %slice.680) | copy-start | bytes 6148
  73.9 22.7 %copy-start.60 = (f32[1,512]{1,0:T(1,128)}, f32[1,512]{1,0:T(1,128)S(1)}, u32[]{:S(2)}) copy-start(f32[1,512]{1,0:T(1,128)S(1)} %slice.676) | copy-start | bytes 6148
  74.0 22.7 %copy-start.64 = (f32[1,512]{1,0:T(1,128)}, f32[1,512]{1,0:T(1,128)S(1)}, u32[]{:S(2)}) copy-start(f32[1,512]{1,0:T(1,128)S(1)} %slice.674) | copy-start | bytes 6148
  74.7 22.0 %copy-start.66 = (f32[1,512]{1,0:T(1,128)}, f32[1,512]{1,0:T(1,128)S(1)}, u32[]{:S(2)}) copy-start(f32[1,512]{1,0:T(1,128)S(1)} %slice.672) | copy-start | bytes 6148
  74.9 21.9 %copy-start.68 = (f32[1,512]{1,0:T(1,128)}, f32[1,512]{1,0:T(1,128)S(1)}, u32[]{:S(2)}) copy-start(f32[1,512]{1,0:T(1,128)S(1)} %slice.670) | copy-start | bytes 6148
  75.6 21.2 %copy-start.70 = (f32[1,512]{1,0:T(1,128)}, f32[1,512]{1,0:T(1,128)S(1)}, u32[]{:S(2)}) copy-start(f32[1,512]{1,0:T(1,128)S(1)} %slice.668) | copy-start | bytes 6148
  75.7 21.1 %copy-start.72 = (f32[1,512]{1,0:T(1,128)}, f32[1,512]{1,0:T(1,128)S(1)}, u32[]{:S(2)}) copy-start(f32[1,512]{1,0:T(1,128)S(1)} %slice.666) | copy-start | bytes 6148
  76.4 20.4 %copy-start.74 = (f32[1,512]{1,0:T(1,128)}, f32[1,512]{1,0:T(1,128)S(1)}, u32[]{:S(2)}) copy-start(f32[1,512]{1,0:T(1,128)S(1)} %slice.664) | copy-start | bytes 6148
  76.6 20.1 %copy-start.62 = (f32[1,512]{1,0:T(1,128)}, f32[1,512]{1,0:T(1,128)S(1)}, u32[]{:S(2)}) copy-start(f32[1,512]{1,0:T(1,128)S(1)} %slice.706) | copy-start | bytes 6148
  77.3 19.5 %copy-start.76 = (f32[1,512]{1,0:T(1,128)}, f32[1,512]{1,0:T(1,128)S(1)}, u32[]{:S(2)}) copy-start(f32[1,512]{1,0:T(1,128)S(1)} %slice.662) | copy-start | bytes 6148
  77.3 0.8 copy-start.1
  77.4 19.4 %copy-start.78 = (f32[1,512]{1,0:T(1,128)}, f32[1,512]{1,0:T(1,128)S(1)}, u32[]{:S(2)}) copy-start(f32[1,512]{1,0:T(1,128)S(1)} %slice.660) | copy-start | bytes 6148
  78.1 18.7 %copy-start.80 = (f32[1,512]{1,0:T(1,128)}, f32[1,512]{1,0:T(1,128)S(1)}, u32[]{:S(2)}) copy-start(f32[1,512]{1,0:T(1,128)S(1)} %slice.658) | copy-start | bytes 6148
  78.3 18.6 %copy-start.82 = (f32[1,512]{1,0:T(1,128)}, f32[1,512]{1,0:T(1,128)S(1)}, u32[]{:S(2)}) copy-start(f32[1,512]{1,0:T(1,128)S(1)} %slice.656) | copy-start | bytes 6148
  78.4 18.5 %copy-start.84 = (f32[1,512]{1,0:T(1,128)}, f32[1,512]{1,0:T(1,128)S(1)}, u32[]{:S(2)}) copy-start(f32[1,512]{1,0:T(1,128)S(1)} %slice.654) | copy-start | bytes 6148
  118.8 21.3 %copy-start.81 = (f32[1,512]{1,0:T(1,128)S(1)}, f32[1,512]{1,0:T(1,128)}, u32[]{:S(2)}) copy-start(f32[1,512]{1,0:T(1,128)} %copy-done.80) | copy-start | bytes 6148
  118.8 21.3 %copy-start.83 = (f32[1,512]{1,0:T(1,128)S(1)}, f32[1,512]{1,0:T(1,128)}, u32[]{:S(2)}) copy-start(f32[1,512]{1,0:T(1,128)} %copy-done.82) | copy-start | bytes 6148
  118.8 21.3 %copy-start.85 = (f32[1,512]{1,0:T(1,128)S(1)}, f32[1,512]{1,0:T(1,128)}, u32[]{:S(2)}) copy-start(f32[1,512]{1,0:T(1,128)} %copy-done.84) | copy-start | bytes 6148
  118.8 22.2 %copy-start.35 = (f32[1,512]{1,0:T(1,128)S(1)}, f32[1,512]{1,0:T(1,128)}, u32[]{:S(2)}) copy-start(f32[1,512]{1,0:T(1,128)} %copy-done.34) | copy-start | bytes 6148
  183.3 49.8 %copy-start.27 = (f32[59,512]{1,0:T(8,128)S(1)}, f32[59,512]{1,0:T(8,128)}, u32[]{:S(2)}) copy-start(f32[59,512]{1,0:T(8,128)} %param.19) | copy-start | bytes 362500
  184.1 49.0 %copy-start.26 = (f32[59,512]{1,0:T(8,128)S(1)}, f32[59,512]{1,0:T(8,128)}, u32[]{:S(2)}) copy-start(f32[59,512]{1,0:T(8,128)} %param.18) | copy-start | bytes 362500
  184.1 49.0 %copy-start.94 = (f32[59]{0:T(128)S(1)}, f32[59]{0:T(128)}, u32[]{:S(2)}) copy-start(f32[59]{0:T(128)} %constant.371.clone.1) | copy-start | bytes 712
  (54 other events, 39.5 us)
Sparse Core Ops, SparseCore 0:
  184.3 48.7 all-reduce.75
where the time goes:
time: 246 us; the launch traced here: 242 us
  waiting for transfers between devices  63.3 us (26%)
  other arithmetic  55 us (22%)
  local copies, waits for them, and re-layouts  52.9 us (22%)
  blocking collectives  23 us (9%)
  starting transfers between devices  19.7 us (8%)
  between operations  15.7 us (6%)
  loops' own time  8.93 us (4%)
  matrix products  3.29 us (1%)
    psum x1, waiting for transfers between devices, body(): total = lax.psum(grads, 'view')  49 us
    all_to_all x1, blocking collectives, body(): lax.all_to_all(slot_grad, 'gauss', split_axis=1, concat_axis=1, tiled=True)  23 us
    all_to_all x1, starting transfers between devices, body(): lax.all_to_all(picked, 'gauss', split_axis=1, concat_axis=1, tiled=True)  19.4 us
    slice x50, local copies, waits for them, and re-layouts, project(): total = total + basis[order] * columns[11 + 3 * order + channel]  16.8 us
    all_to_all x1, waiting for transfers between devices, body(): lax.all_to_all(picked, 'gauss', split_axis=1, concat_axis=1, tiled=True)  14.3 us
    unnamed x212, local copies, waits for them, and re-layouts  14.1 us
    another operation x24, other arithmetic  8.63 us
    add_any x2, other arithmetic, project(): quat_z * quat_z  7.79 us
  transfers between devices with their start and end apart: 2, of which 2 were waited for; matrix products, arithmetic and copies ran while one was open for 0% of the time, Pallas kernels for 0%

commit v1 on v0

v1 whole, which is shorter than its diff:
```python
import jax
import jax.numpy as jnp
from jax import lax
from jax.experimental import pallas as pl
from jax.experimental.pallas import tpu as pltpu
from jax.sharding import PartitionSpec as P

focal_length = 1100.0
centre_x = 960.0
centre_y = 540.0
beta_one = 0.9
beta_two = 0.999
adam_eps = 1e-15
adam_step = 100.0
log2_e = 1.4426950408889634
sh_zero = 0.28209479177387814
sh_one = 0.4886025119029199
sh_two = [
    1.0925484305920792,
    -1.0925484305920792,
    0.31539156525252005,
    -1.0925484305920792,
    0.5462742152960396,
]
sh_three = [
    -0.5900435899266435,
    2.890611442640554,
    -0.4570457994644658,
    0.3731763325901154,
    -0.4570457994644658,
    1.445305721320277,
    -0.5900435899266435,
]
LINE = 16
GROUP = 8
VIEWS = 4
MESH = pl.DeviceIdType.MESH
f32 = jnp.float32
bf16 = jnp.bfloat16


def harmonics(dir_x, dir_y, dir_z):
    sq_x = dir_x * dir_x
    sq_y = dir_y * dir_y
    sq_z = dir_z * dir_z
    return [
        -sh_one * dir_y,
        sh_one * dir_z,
        -sh_one * dir_x,
        sh_two[0] * dir_x * dir_y,
        sh_two[1] * dir_y * dir_z,
        sh_two[2] * (2.0 * sq_z - sq_x - sq_y),
        sh_two[3] * dir_x * dir_z,
        sh_two[4] * (sq_x - sq_y),
        sh_three[0] * dir_y * (3.0 * sq_x - sq_y),
        sh_three[1] * dir_x * dir_y * dir_z,
        sh_three[2] * dir_y * (4.0 * sq_z - sq_x - sq_y),
        sh_three[3] * dir_z * (2.0 * sq_z - 3.0 * sq_x - 3.0 * sq_y),
        sh_three[4] * dir_x * (4.0 * sq_z - sq_x - sq_y),
        sh_three[5] * dir_z * (sq_x - sq_y),
        sh_three[6] * dir_x * (sq_x - 3.0 * sq_y),
    ]


def project(columns, camera):
    mean_x, mean_y, mean_z = columns[0], columns[1], columns[2]
    scales = [jnp.exp(columns[3 + axis]) for axis in range(3)]
    quat_w, quat_x, quat_y, quat_z = columns[6:10]
    norm = 1.0 / jnp.sqrt(quat_w * quat_w + quat_x * quat_x + quat_y * quat_y + quat_z * quat_z)
    quat_w, quat_x, quat_y, quat_z = quat_w * norm, quat_x * norm, quat_y * norm, quat_z * norm
    turn = [
        [
            1.0 - 2.0 * (quat_y * quat_y + quat_z * quat_z),
            2.0 * (quat_x * quat_y - quat_w * quat_z),
            2.0 * (quat_x * quat_z + quat_w * quat_y),
        ],
        [
            2.0 * (quat_x * quat_y + quat_w * quat_z),
            1.0 - 2.0 * (quat_x * quat_x + quat_z * quat_z),
            2.0 * (quat_y * quat_z - quat_w * quat_x),
        ],
        [
            2.0 * (quat_x * quat_z - quat_w * quat_y),
            2.0 * (quat_y * quat_z + quat_w * quat_x),
            1.0 - 2.0 * (quat_x * quat_x + quat_y * quat_y),
        ],
    ]
    world = [[turn[outer][inner] * scales[inner] for inner in range(3)] for outer in range(3)]
    cam_x, cam_y, depth = [
        camera[3 * outer] * mean_x
        + camera[3 * outer + 1] * mean_y
        + camera[3 * outer + 2] * mean_z
        + camera[9 + outer]
        for outer in range(3)
    ]
    framed = [
        [
            camera[3 * outer] * world[0][inner]
            + camera[3 * outer + 1] * world[1][inner]
            + camera[3 * outer + 2] * world[2][inner]
            for inner in range(3)
        ]
        for outer in range(3)
    ]
    inverse = 1.0 / depth
    near = focal_length * inverse
    slope_x = cam_x * inverse
    slope_y = cam_y * inverse
    row_top = [near * (framed[0][inner] - slope_x * framed[2][inner]) for inner in range(3)]
    row_low = [near * (framed[1][inner] - slope_y * framed[2][inner]) for inner in range(3)]
    cov_a = row_top[0] * row_top[0] + row_top[1] * row_top[1] + row_top[2] * row_top[2] + 0.3
    cov_b = row_top[0] * row_low[0] + row_top[1] * row_low[1] + row_top[2] * row_low[2]
    cov_c = row_low[0] * row_low[0] + row_low[1] * row_low[1] + row_low[2] * row_low[2] + 0.3
    over = 1.0 / (cov_a * cov_c - cov_b * cov_b)
    centre_u = focal_length * slope_x + centre_x
    centre_v = focal_length * slope_y + centre_y
    away = 1.0 / jnp.sqrt(cam_x * cam_x + cam_y * cam_y + depth * depth)
    basis = harmonics(cam_x * away, cam_y * away, depth * away)
    colours = []
    for channel in range(3):
        total = 0.5 + sh_zero * columns[11 + channel]
        for order in range(15):
            total = total + basis[order] * columns[14 + 3 * order + channel]
        colours.append(total)
    opacity = 1.0 / (1.0 + jnp.exp(-columns[10]))
    return [
        centre_u,
        centre_v,
        cov_c * over,
        -cov_b * over,
        cov_a * over,
        opacity,
        colours[0],
        colours[1],
        colours[2],
    ]


def pieces(value):
    high = value.astype(bf16)
    rest = value - high.astype(f32)
    middle = rest.astype(bf16)
    low = (rest - middle.astype(f32)).astype(bf16)
    return high, middle, low


def dot_rows(left, right):
    return lax.dot_general(left, right, (((1,), (1,)), ((), ())), preferred_element_type=f32)


def dot_exact(left, right):
    high, middle, low = pieces(left)
    return (
        jnp.dot(high, right, preferred_element_type=f32)
        + jnp.dot(middle, right, preferred_element_type=f32)
    ) + jnp.dot(low, right, preferred_element_type=f32)


def dot_rows_exact(left, right):
    high, middle, low = pieces(left)
    return (dot_rows(high, right) + dot_rows(middle, right)) + dot_rows(low, right)


def iota(shape, axis):
    return lax.broadcasted_iota(jnp.int32, shape, axis)


def one_hot(test):
    return jnp.where(test, 1.0, 0.0).astype(bf16)


def swap(value):
    return pltpu.roll(value, 64, 1)


def reorder_row(row, width, place):
    split = jnp.concatenate([row >> 4, row & 15, jnp.zeros((6, width), jnp.int32)], axis=0)
    chosen = one_hot(iota((width, width), 0) == place(iota((width, width), 1)))
    moved = jnp.dot(split.astype(f32).astype(bf16), chosen, preferred_element_type=f32)
    return (moved[0:1] * 16.0 + moved[1:2]).astype(jnp.int32)


def sender_table(rows):
    moved = reorder_row(rows, 512, lambda n: 8 * (n & 63) + (n >> 6))
    return one_hot(iota((512, 512), 0) == moved)


def pack_messages(attributes, table):
    placed = dot_exact(attributes, table)
    parts = []
    for pair in range(4):
        both = placed[:, 128 * pair : 128 * pair + 128]
        parts += [both, swap(both)]
    return jnp.transpose(jnp.concatenate(parts, axis=0))[0:64]


def unpack_messages(messages, table):
    turned = jnp.transpose(jnp.concatenate([messages, jnp.zeros_like(messages)], axis=0))
    keep = iota((16, 128), 1) < 64
    parts = []
    for pair in range(4):
        left = turned[32 * pair : 32 * pair + 16]
        right = turned[32 * pair + 16 : 32 * pair + 32]
        parts.append(jnp.where(keep, left, swap(right)))
    return dot_rows_exact(jnp.concatenate(parts, axis=1), table)


def list_tables(lists):
    moved = []
    for tile in range(2):
        moved.append(reorder_row(lists[tile : tile + 1], 256, lambda n: 32 * (n & 7) + (n >> 3)))
    slot = jnp.concatenate(moved, axis=1)
    sender = slot >> 2
    line = sender >> 3
    row = (sender & 7) * 8 + (line & 7)
    group = (line >> 3) * 4 + (slot & 3)
    return one_hot(iota((64, 512), 0) == row), group


def pick(received, table, group):
    turned = jnp.transpose(jnp.concatenate([received, jnp.zeros_like(received)], axis=0))[:, 0:64]
    found = dot_exact(turned, table)
    found = jnp.where((iota((128, 512), 0) >> 4) == group, found, 0.0)
    total = found[0:16]
    for part in range(1, 8):
        total = total + found[16 * part : 16 * part + 16]
    return total


def unpick(grads, table, group):
    spread = jnp.concatenate([grads] * 8, axis=0)
    spread = jnp.where((iota((128, 512), 0) >> 4) == group, spread, 0.0)
    turned = dot_rows_exact(spread, table)
    return jnp.transpose(jnp.concatenate([turned, jnp.zeros((128, 64), f32)], axis=1))[0:64]


def place_of(position):
    return 32 * (position & 7) + (position >> 3)


def prepare_tile(attributes, count, tile_id):
    across = (16 * lax.rem(tile_id, 120)).astype(f32) + 7.5
    down = (16 * lax.div(tile_id, 120)).astype(f32) + 7.5
    centre_u = attributes[0:1] - across
    centre_v = attributes[1:2] - down
    alive = place_of(iota((1, 256), 1)) < count
    rows = [
        centre_u,
        centre_v,
        attributes[2:3] * (-0.5 * log2_e),
        attributes[3:4] * (-log2_e),
        attributes[4:5] * (-0.5 * log2_e),
        jnp.where(alive, attributes[5:6], 0.0),
        attributes[6:7],
        attributes[7:8],
        attributes[8:9],
        jnp.zeros((119, 256), f32),
    ]
    return jnp.transpose(jnp.concatenate(rows, axis=0)), centre_u, centre_v


def pixels():
    number = iota((1, 256), 1)
    return (number & 15).astype(f32) - 7.5, (number >> 4).astype(f32) - 7.5


def shade_step(columns, pixel_x, pixel_y, carry):
    keep, colour = carry
    offset_x = pixel_x - columns[:, 0:1]
    offset_y = pixel_y - columns[:, 1:2]
    power = offset_x * (columns[:, 2:3] * offset_x + columns[:, 3:4] * offset_y) + (
        columns[:, 4:5] * offset_y
    ) * offset_y
    alpha = columns[:, 5:6] * jnp.exp2(power)
    weight = keep * alpha
    colour = [colour[c] + weight * columns[:, 6 + c : 7 + c] for c in range(3)]
    return alpha, weight, (keep * (1.0 - alpha), colour)


def between(keep, colour, target):
    before = [jnp.ones((1, 256), f32)]
    for chunk in range(7):
        before.append(before[-1] * keep[chunk : chunk + 1])
    before = jnp.concatenate(before, axis=0)
    colour = [part * before for part in colour]
    residual = [jnp.sum(colour[c], axis=0, keepdims=True) - target[c : c + 1] for c in range(3)]
    own = residual[0] * colour[0] + residual[1] * colour[1] + residual[2] * colour[2]
    after = [jnp.zeros((1, 256), f32)]
    for chunk in range(7, 0, -1):
        after.append(after[-1] + own[chunk : chunk + 1])
    after = jnp.concatenate(after[::-1], axis=0)
    squares = residual[0] * residual[0] + residual[1] * residual[1] + residual[2] * residual[2]
    return before, after, residual, 0.5 * jnp.sum(squares, axis=1, keepdims=True)


def back_step(columns, alpha, weight, before, after, residual, later):
    shade = (
        residual[0] * columns[:, 6:7] + residual[1] * columns[:, 7:8] + residual[2] * columns[:, 8:9]
    )
    own = weight * shade
    ratio = alpha / (1.0 - alpha)
    slope = before * (own - later * ratio) - after * ratio
    return slope, before * weight, later + own


def moments(slope, weight, residual):
    pixel_x, pixel_y = pixels()
    ones = jnp.ones((1, 256), f32)
    powers = [ones, pixel_x, pixel_y, pixel_x * pixel_x, pixel_x * pixel_y, pixel_y * pixel_y]
    powers = jnp.concatenate(powers + [jnp.zeros((122, 256), f32)], axis=0).astype(bf16)
    shown = jnp.concatenate(
        [jnp.zeros((6, 256), f32)] + residual + [jnp.zeros((119, 256), f32)], axis=0
    )
    high, middle, low = pieces(shown)
    first, second, third = pieces(weight)
    total = dot_rows_exact(slope, powers)
    total = total + (dot_rows(first, high) + (dot_rows(first, middle) + dot_rows(second, high)))
    total = total + (dot_rows(first, low) + (dot_rows(second, middle) + dot_rows(third, high)))
    return jnp.transpose(total)[0:16]


def finish_tile(sums, attributes, centre_u, centre_v):
    whole, by_x, by_y, by_xx, by_xy, by_yy = [sums[n : n + 1] for n in range(6)]
    sum_x = by_x - centre_u * whole
    sum_y = by_y - centre_v * whole
    sum_xx = by_xx - centre_u * (by_x + sum_x)
    sum_xy = by_xy - centre_u * by_y - centre_v * sum_x
    sum_yy = by_yy - centre_v * (by_y + sum_y)
    conic = [attributes[2 + n : 3 + n] for n in range(3)]
    rows = [
        conic[0] * sum_x + conic[1] * sum_y,
        conic[1] * sum_x + conic[2] * sum_y,
        -0.5 * sum_xx,
        -sum_xy,
        -0.5 * sum_yy,
        whole,
        sums[6:9],
        jnp.zeros((7, 256), f32),
    ]
    return jnp.concatenate(rows, axis=0)


def exchange(
    params,
    camera,
    rows,
    lists,
    counts,
    tile_ids,
    target,
    out,
    loss,
    msg,
    land1,
    pass1,
    land2,
    back1,
    land3,
    pass2,
    land4,
    own,
    land5,
    columns,
    alphas,
    weights,
    table,
    send1,
    recv1,
    send2,
    recv2,
    send3,
    recv3,
    send4,
    recv4,
    send5,
    recv5,
):
    here = lax.axis_index("gauss")
    view = lax.axis_index("view")
    line = here // GROUP
    group = lax.rem(here, GROUP)

    def on_line(step):
        other = lax.rem(line + step, LINE)
        return other, {"gauss": other * GROUP + group, "view": view}

    def in_group(step):
        other = lax.rem(group + step, GROUP)
        return other, {"gauss": line * GROUP + other, "view": view}

    def over_views(step):
        other = lax.rem(view + step, VIEWS)
        return other, {"gauss": here, "view": other}

    def each(peers, count, action):
        def one(step, unused):
            action(step, *peers(step))
            return unused

        lax.fori_loop(1, count, one, 0)

    barrier = pltpu.get_barrier_semaphore()

    def greet(step, other, device):
        pl.semaphore_signal(barrier, inc=1, device_id=device, device_id_type=MESH)

    each(on_line, LINE, greet)
    each(in_group, GROUP, greet)
    each(over_views, VIEWS, greet)

    def swap_blocks(peers, count, mine, source, target_buffer, sent, arrived):
        def copy(step, other, device):
            return pltpu.make_async_remote_copy(
                src_ref=source.at[other],
                dst_ref=target_buffer.at[mine],
                send_sem=sent.at[step],
                recv_sem=arrived.at[mine],
                device_id=device,
                device_id_type=MESH,
            )

        def wait(step, other, device):
            pltpu.make_async_remote_copy(
                src_ref=source.at[other],
                dst_ref=target_buffer.at[other],
                send_sem=sent.at[step],
                recv_sem=arrived.at[other],
                device_id=device,
                device_id_type=MESH,
            ).wait()

        each(peers, count, lambda *peer: copy(*peer).start())
        target_buffer[mine] = source[mine]
        return lambda: each(peers, count, wait)

    table[...] = sender_table(rows[...])
    scalars = [camera[0, n] for n in range(12)]
    attributes = project([params[n : n + 1, :] for n in range(59)], scalars)
    messages = pack_messages(
        jnp.concatenate(attributes + [jnp.zeros((7, 512), f32)], axis=0), table[...]
    )
    msg[...] = messages.reshape(LINE, 4, 128)

    pl.semaphore_wait(barrier, LINE + GROUP + VIEWS - 3)
    arrive = swap_blocks(on_line, LINE, line, msg, land1, send1, recv1)
    picked, lane_group = list_tables(lists[0])
    arrive()
    low_lanes = iota((8, 128), 1) < 64
    for pair in range(4):
        lower, upper = land1[0:8, pair, :], land1[8:16, pair, :]
        pass1[2 * pair] = jnp.where(low_lanes, lower, swap(upper))
        pass1[2 * pair + 1] = jnp.where(low_lanes, swap(lower), upper)
    arrive = swap_blocks(in_group, GROUP, group, pass1, land2, send2, recv2)
    arrive()

    found = pick(land2[...].reshape(64, 128), picked, lane_group)
    pixel_x, pixel_y = pixels()
    centres = []
    for tile in range(2):
        entries = found[:, 256 * tile : 256 * tile + 256]
        filled, centre_u, centre_v = prepare_tile(entries, counts[0, tile], tile_ids[0, tile])
        columns[tile] = filled
        centres.append((entries, centre_u, centre_v))

    def forward(step, carry):
        rows_here = pl.ds(pl.multiple_of(step * 8, 8), 8)
        left = []
        for tile in range(2):
            alpha, weight, rest = shade_step(
                columns[tile, rows_here, :], pixel_x, pixel_y, carry[tile]
            )
            alphas[tile, rows_here, :] = alpha
            weights[tile, rows_here, :] = weight
            left.append(rest)
        return left

    fresh = (jnp.ones((8, 256), f32), [jnp.zeros((8, 256), f32)] * 3)
    carry = lax.fori_loop(0, 32, forward, [fresh, fresh], unroll=4)
    around = []
    for tile in range(2):
        around.append(between(carry[tile][0], carry[tile][1], target[0, tile]))
    spot = iota((1, 128), 1)
    loss[...] = jnp.where(spot == 0, around[0][3], jnp.where(spot == 1, around[1][3], 0.0))

    def backward(step, later):
        rows_here = pl.ds(pl.multiple_of((31 - step) * 8, 8), 8)
        left = []
        for tile in range(2):
            before, after, residual, unused = around[tile]
            slope, weight, rest = back_step(
                columns[tile, rows_here, :],
                alphas[tile, rows_here, :],
                weights[tile, rows_here, :],
                before,
                after,
                residual,
                later[tile],
            )
            alphas[tile, rows_here, :] = slope
            weights[tile, rows_here, :] = weight
            left.append(rest)
        return left

    lax.fori_loop(0, 32, backward, [jnp.zeros((8, 256), f32)] * 2, unroll=4)
    grads = []
    for tile in range(2):
        sums = moments(alphas[tile], weights[tile], around[tile][2])
        grads.append(finish_tile(sums, *centres[tile]))
    grads = jnp.concatenate(grads, axis=1)
    back1[...] = unpick(grads, picked, lane_group).reshape(GROUP, 8, 128)

    arrive = swap_blocks(in_group, GROUP, group, back1, land3, send3, recv3)
    arrive()
    for pair in range(4):
        even, odd = land3[2 * pair], land3[2 * pair + 1]
        pass2[0:8, pair, :] = jnp.where(low_lanes, even, swap(odd))
        pass2[8:16, pair, :] = jnp.where(low_lanes, swap(even), odd)
    arrive = swap_blocks(on_line, LINE, line, pass2, land4, send4, recv4)
    arrive()
    returned = unpack_messages(land4[...].reshape(64, 128), table[...])

    lanes = iota((1, 512), 1)
    pose = jnp.zeros((1, 512), f32)
    for n in range(12):
        pose = jnp.where(lanes == n, scalars[n], pose)
    own[...] = jnp.concatenate([returned[0:9], pose, jnp.zeros((6, 512), f32)], axis=0)

    def share(step, other, device):
        return pltpu.make_async_remote_copy(
            src_ref=own,
            dst_ref=land5.at[view],
            send_sem=send5.at[step],
            recv_sem=recv5.at[view],
            device_id=device,
            device_id_type=MESH,
        )

    def take(step, other, device):
        pltpu.make_async_remote_copy(
            src_ref=own,
            dst_ref=land5.at[other],
            send_sem=send5.at[step],
            recv_sem=recv5.at[other],
            device_id=device,
            device_id_type=MESH,
        ).wait()

    each(over_views, VIEWS, lambda *peer: share(*peer).start())
    land5[view] = own[...]
    each(over_views, VIEWS, take)
    out[...] = land5[...]


def update(params, first, second, grads, loss, new_params, new_first, new_second, tile_loss, whole):
    columns = [jnp.broadcast_to(params[n : n + 1, :], (VIEWS, 512)) for n in range(59)]
    camera = [grads[:, 9, n : n + 1] for n in range(12)]
    attributes, back = jax.vjp(lambda rows: project(rows, camera)[0:5] + project(rows, camera)[6:9], columns)
    given = [grads[:, n, :] for n in range(9)]
    pulled = back(given[0:5] + given[6:9])[0]
    opacity = 1.0 / (1.0 + jnp.exp(-columns[10]))
    pulled[10] = given[5] * (1.0 - opacity)
    for n in range(59):
        whole[n : n + 1, :] = jnp.sum(pulled[n], axis=0, keepdims=True)
    total = whole[...]
    row = iota((59, 1), 0)
    rate = jnp.where(row < 3, 0.00016, 0.005)
    rate = jnp.where(row < 6, rate, 0.001)
    rate = jnp.where(row < 10, rate, 0.05)
    rate = jnp.where(row < 11, rate, 0.0025)
    rate = jnp.where(row < 14, rate, 0.000125)
    rate = rate / (1.0 - beta_one**adam_step)
    moved = beta_one * first[...] + (1.0 - beta_one) * total
    spread = beta_two * second[...] + (1.0 - beta_two) * total * total
    new_first[...] = moved
    new_second[...] = spread
    new_params[...] = params[...] - rate * moved / (
        jnp.sqrt(spread / (1.0 - beta_two**adam_step)) + adam_eps
    )
    tile_loss[...] = loss[:, 0:2]


def body(params, first_moment, second_moment, cameras, send_rows, lists, counts, tile_ids, target):
    vmem = pl.BlockSpec(memory_space=pltpu.VMEM)
    smem = pl.BlockSpec(memory_space=pltpu.SMEM)
    dma = pltpu.SemaphoreType.DMA
    grads, loss = pl.pallas_call(
        exchange,
        out_shape=(
            jax.ShapeDtypeStruct((VIEWS, 16, 512), f32),
            jax.ShapeDtypeStruct((1, 128), f32),
        ),
        in_specs=[vmem, smem, vmem, vmem, smem, smem, vmem],
        out_specs=(vmem, vmem),
        scratch_shapes=[
            pltpu.VMEM((LINE, 4, 128), f32),
            pltpu.VMEM((LINE, 4, 128), f32),
            pltpu.VMEM((GROUP, 8, 128), f32),
            pltpu.VMEM((GROUP, 8, 128), f32),
            pltpu.VMEM((GROUP, 8, 128), f32),
            pltpu.VMEM((GROUP, 8, 128), f32),
            pltpu.VMEM((LINE, 4, 128), f32),
            pltpu.VMEM((LINE, 4, 128), f32),
            pltpu.VMEM((16, 512), f32),
            pltpu.VMEM((VIEWS, 16, 512), f32),
            pltpu.VMEM((2, 256, 128), f32),
            pltpu.VMEM((2, 256, 256), f32),
            pltpu.VMEM((2, 256, 256), f32),
            pltpu.VMEM((512, 512), bf16),
            dma((LINE,)),
            dma((LINE,)),
            dma((GROUP,)),
            dma((GROUP,)),
            dma((GROUP,)),
            dma((GROUP,)),
            dma((LINE,)),
            dma((LINE,)),
            dma((VIEWS,)),
            dma((VIEWS,)),
        ],
        compiler_params=pltpu.CompilerParams(
            collective_id=0, has_side_effects=True, vmem_limit_bytes=32 * 1024 * 1024
        ),
        name="exchange",
    )(params, cameras, send_rows.reshape(1, 512), lists, counts, tile_ids, target)
    whole = jax.ShapeDtypeStruct((59, 512), f32)
    return pl.pallas_call(
        update,
        out_shape=(whole, whole, whole, jax.ShapeDtypeStruct((1, 2), f32)),
        in_specs=[vmem] * 5,
        out_specs=(vmem,) * 4,
        scratch_shapes=[pltpu.VMEM((59, 512), f32)],
        compiler_params=pltpu.CompilerParams(vmem_limit_bytes=32 * 1024 * 1024),
        name="update",
    )(params, first_moment, second_moment, grads, loss)


def solution(mesh):
    in_specs = (
        P(None, "gauss"),
        P(None, "gauss"),
        P(None, "gauss"),
        P("view", None),
        P("view", "gauss", None),
        P("view", "gauss", None),
        P("view", "gauss"),
        P("view", "gauss"),
        P("view", "gauss", None, None),
    )
    out_specs = (P(None, "gauss"), P(None, "gauss"), P(None, "gauss"), P("view", "gauss"))
    return jax.shard_map(body, mesh=mesh, in_specs=in_specs, out_specs=out_specs, check_vma=False)
```

time: 246 us -> 55.3 us (0.22)
  the two profiles are of different devices: /device:TPU:6 before, /device:TPU:1 now
where the time goes in v1:
time: 55.3 us; the launch traced here: 55.1 us
  Pallas kernels  51.8 us (94%)
  local copies, waits for them, and re-layouts  2.55 us (5%)
  between operations  0.73 us (1%)
    pallas_call x1, Pallas kernels, body(): pl.pallas_call(exchange, out_shape=(jax.ShapeDtypeStruct((VIEWS, 16, 512)...  50.2 us
    unnamed x17, local copies, waits for them, and re-layouts  2.55 us
    pallas_call x1, Pallas kernels, body(): pl.pallas_call(update, out_shape=(whole, whole, whole, jax.ShapeDtypeStru...  1.61 us

profile of v1, /device:TPU:1, one launch (start us, length us, event | category | flops | bytes accessed | tf_op | source)
XLA Modules:
  0.0 55.1 jit_solution(8763141659814818736)
XLA Ops:
  0.6 0.0 copy-start.3
  0.6 0.0 copy-start.4
  0.7 0.0 copy-start.5
  0.7 0.0 copy-start.6
  0.7 0.0 copy-start.7
  0.7 0.7 %copy.13.target = f32[1,2,3,256]{3,2,1,0:T(4,128)S(1)} copy(f32[1,2,3,256]{3,1,2,0:T(2,128)} %param.17) | data formatting | bytes 12288 | tf_op args[8]
  1.4 0.0 copy-done.3
  1.4 0.0 copy-done.4
  1.4 0.0 copy-done.5
  1.4 0.0 copy-done.6
  1.4 0.0 copy-done.7
  1.4 0.0 copy-start
  1.4 0.9 %copy-done = f32[59,512]{1,0:T(8,128)S(1)} copy-done((f32[59,512]{1,0:T(8,128)S(1)}, f32[59,512]{1,0:T(8,128)}, u32[]{:S(2)}) %copy-start) | copy-done | bytes 120856
  2.3 0.0 copy-start.1
  2.3 50.2 %exchange.1 = (f32[4,16,512]{2,1,0:T(8,128)S(1)}, f32[1,128]{1,0:T(1,128)S(1)}) custom-call(f32[59,512]{1,0:T(8,128)S(1)} %copy-done, f32[1,12]{1,0:T(1,128)S(1)} %copy-done.5, s32[1,512]{1,0:T(1,128)S(1)} %bitcast.1, s32[1,2,256]{2,1,0:T(2,128)S(1)} %copy-done.4, s32[1,2]{1,0:T(1,128)S(1)} %copy-done.6, s32[1,2]{1,0:T(1,128)S(1)} %copy-done.7, ...), custom_call_target="tpu_custom_call" | custom-call | tf_op jit(solution)/shard_map/exchange/pallas_call | solution.py:586
  52.6 0.0 copy-done.1
  52.6 0.0 copy-start.2
  52.6 0.9 %copy-done.2 = f32[59,512]{1,0:T(8,128)S(1)} copy-done((f32[59,512]{1,0:T(8,128)S(1)}, f32[59,512]{1,0:T(8,128)}, u32[]{:S(2)}) %copy-start.2) | copy-done | bytes 120856
  53.5 1.6 %update.1 = (f32[59,512]{1,0:T(8,128)}, f32[59,512]{1,0:T(8,128)}, f32[59,512]{1,0:T(8,128)}, f32[1,2]{1,0:T(1,128)}) custom-call(f32[59,512]{1,0:T(8,128)S(1)} %copy-done, f32[59,512]{1,0:T(8,128)S(1)} %copy-done.1, f32[59,512]{1,0:T(8,128)S(1)} %copy-done.2, f32[4,16,512]{2,1,0:T(8,128)S(1)} %get-tuple-element.6.grads, f32[1,128]{1,0:T(1,128)S(1)} %get-tuple-element.7.loss), custom_call_target="tpu_custom_call" | custom-call | tf_op jit(solution)/shard_map/update/pallas_call | solution.py:626
Async XLA Ops:
  0.6 0.8 %copy-start.3 = (s32[1,1,512]{2,1,0:T(1,128)S(1)}, s32[1,1,512]{2,1,0:T(1,128)}, u32[]{:S(2)}) copy-start(s32[1,1,512]{2,1,0:T(1,128)} %param.13) | copy-start | bytes 6148
  0.6 0.8 %copy-start.4 = (s32[1,2,256]{2,1,0:T(2,128)S(1)}, s32[1,2,256]{2,1,0:T(2,128)}, u32[]{:S(2)}) copy-start(s32[1,2,256]{2,1,0:T(2,128)} %lists.1) | copy-start | bytes 6148
  0.7 0.8 %copy-start.5 = (f32[1,12]{1,0:T(1,128)S(1)}, f32[1,12]{1,0:T(1,128)}, u32[]{:S(2)}) copy-start(f32[1,12]{1,0:T(1,128)} %camera.1) | copy-start | bytes 148
  0.7 0.8 %copy-start.6 = (s32[1,2]{1,0:T(1,128)S(1)}, s32[1,2]{1,0:T(1,128)}, u32[]{:S(2)}) copy-start(s32[1,2]{1,0:T(1,128)} %counts.1) | copy-start | bytes 28
  0.7 0.8 %copy-start.7 = (s32[1,2]{1,0:T(1,128)S(1)}, s32[1,2]{1,0:T(1,128)}, u32[]{:S(2)}) copy-start(s32[1,2]{1,0:T(1,128)} %tile_ids.1) | copy-start | bytes 28
  1.4 0.9 %copy-start = (f32[59,512]{1,0:T(8,128)S(1)}, f32[59,512]{1,0:T(8,128)}, u32[]{:S(2)}) copy-start(f32[59,512]{1,0:T(8,128)} %params.3) | copy-start | bytes 362500
  2.3 50.2 %copy-start.1 = (f32[59,512]{1,0:T(8,128)S(1)}, f32[59,512]{1,0:T(8,128)}, u32[]{:S(2)}) copy-start(f32[59,512]{1,0:T(8,128)} %first.1) | copy-start | bytes 362500
  52.6 0.9 %copy-start.2 = (f32[59,512]{1,0:T(8,128)S(1)}, f32[59,512]{1,0:T(8,128)}, u32[]{:S(2)}) copy-start(f32[59,512]{1,0:T(8,128)} %second.1) | copy-start | bytes 362500

commit v2 on v1

--- a/solution.py
+++ b/solution.py
@@ -32,7 +32,8 @@
     -0.5900435899266435,
 ]
 LINE = 16
-GROUP = 8
+SIDE = 4
+CHIPS = LINE * SIDE
 VIEWS = 4
 MESH = pl.DeviceIdType.MESH
 f32 = jnp.float32
@@ -148,17 +149,18 @@
     return lax.dot_general(left, right, (((1,), (1,)), ((), ())), preferred_element_type=f32)
 
 
+def add_pieces(stacked):
+    rows = stacked.shape[0] // 3
+    return (stacked[0:rows] + stacked[rows : 2 * rows]) + stacked[2 * rows :]
+
+
 def dot_exact(left, right):
-    high, middle, low = pieces(left)
-    return (
-        jnp.dot(high, right, preferred_element_type=f32)
-        + jnp.dot(middle, right, preferred_element_type=f32)
-    ) + jnp.dot(low, right, preferred_element_type=f32)
+    stacked = jnp.concatenate(pieces(left), axis=0)
+    return add_pieces(jnp.dot(stacked, right, preferred_element_type=f32))
 
 
 def dot_rows_exact(left, right):
-    high, middle, low = pieces(left)
-    return (dot_rows(high, right) + dot_rows(middle, right)) + dot_rows(low, right)
+    return add_pieces(dot_rows(jnp.concatenate(pieces(left), axis=0), right))
 
 
 def iota(shape, axis):
@@ -210,11 +212,7 @@
     for tile in range(2):
         moved.append(reorder_row(lists[tile : tile + 1], 256, lambda n: 32 * (n & 7) + (n >> 3)))
     slot = jnp.concatenate(moved, axis=1)
-    sender = slot >> 2
-    line = sender >> 3
-    row = (sender & 7) * 8 + (line & 7)
-    group = (line >> 3) * 4 + (slot & 3)
-    return one_hot(iota((64, 512), 0) == row), group
+    return one_hot(iota((64, 512), 0) == (slot >> 3)), slot & 7
 
 
 def pick(received, table, group):
@@ -298,7 +296,9 @@
         residual[0] * columns[:, 6:7] + residual[1] * columns[:, 7:8] + residual[2] * columns[:, 8:9]
     )
     own = weight * shade
-    ratio = alpha / (1.0 - alpha)
+    left = 1.0 - alpha
+    guess = pl.reciprocal(left, approx=True)
+    ratio = alpha * (guess * (2.0 - left * guess))
     slope = before * (own - later * ratio) - after * ratio
     return slope, before * weight, later + own
 
@@ -307,16 +307,16 @@
     pixel_x, pixel_y = pixels()
     ones = jnp.ones((1, 256), f32)
     powers = [ones, pixel_x, pixel_y, pixel_x * pixel_x, pixel_x * pixel_y, pixel_y * pixel_y]
-    powers = jnp.concatenate(powers + [jnp.zeros((122, 256), f32)], axis=0).astype(bf16)
-    shown = jnp.concatenate(
-        [jnp.zeros((6, 256), f32)] + residual + [jnp.zeros((119, 256), f32)], axis=0
-    )
-    high, middle, low = pieces(shown)
-    first, second, third = pieces(weight)
-    total = dot_rows_exact(slope, powers)
-    total = total + (dot_rows(first, high) + (dot_rows(first, middle) + dot_rows(second, high)))
-    total = total + (dot_rows(first, low) + (dot_rows(second, middle) + dot_rows(third, high)))
-    return jnp.transpose(total)[0:16]
+    shown = [part.astype(f32) for part in pieces(jnp.concatenate(residual, axis=0))]
+    factors = jnp.concatenate(powers + shown + [jnp.zeros((1, 256), f32)], axis=0).astype(bf16)
+
+    def over_pixels(value):
+        return sum(dot_rows(factors, part) for part in pieces(value)[::-1])
+
+    by_power = over_pixels(slope)[0:6]
+    by_shown = over_pixels(weight)
+    by_shown = by_shown[6:9] + (by_shown[9:12] + by_shown[12:15])
+    return jnp.concatenate([by_power, by_shown], axis=0)
 
 
 def finish_tile(sums, attributes, centre_u, centre_v):
@@ -341,22 +341,32 @@
 
 
 def exchange(
+    params_in,
+    first_in,
+    second_in,
+    camera_in,
+    rows_in,
+    lists_in,
+    counts_in,
+    tile_ids_in,
+    target_in,
     params,
+    first,
+    second,
+    out,
+    loss,
     camera,
     rows,
     lists,
     counts,
     tile_ids,
     target,
-    out,
-    loss,
     msg,
     land1,
-    pass1,
     land2,
     back1,
     land3,
-    pass2,
+    back2,
     land4,
     own,
     land5,
@@ -364,6 +374,7 @@
     alphas,
     weights,
     table,
+    loads,
     send1,
     recv1,
     send2,
@@ -377,83 +388,110 @@
 ):
     here = lax.axis_index("gauss")
     view = lax.axis_index("view")
-    line = here // GROUP
-    group = lax.rem(here, GROUP)
-
-    def on_line(step):
-        other = lax.rem(line + step, LINE)
-        return other, {"gauss": other * GROUP + group, "view": view}
-
-    def in_group(step):
-        other = lax.rem(group + step, GROUP)
-        return other, {"gauss": line * GROUP + other, "view": view}
-
-    def over_views(step):
-        other = lax.rem(view + step, VIEWS)
-        return other, {"gauss": here, "view": other}
-
-    def each(peers, count, action):
+    core = lax.rem(here, 2)
+    chip = here // 2
+    line = chip // SIDE
+    side = lax.rem(chip, SIDE)
+
+    def on_chip(step_z, step_x):
+        other = lax.rem(line + step_z, LINE) * SIDE + lax.rem(side + step_x, SIDE)
+        return other, {"gauss": other * 2 + core, "view": view}
+
+    def far_first(action):
         def one(step, unused):
-            action(step, *peers(step))
+            step_z = LINE // 2 + (1 - 2 * (step & 1)) * ((step + 1) >> 1)
+            for step_x in (2, 1, 3, 0):
+                action(*on_chip(step_z, step_x))
             return unused
 
-        lax.fori_loop(1, count, one, 0)
+        lax.fori_loop(0, LINE - 1, one, 0)
+        for step_x in (2, 1, 3):
+            action(*on_chip(0, step_x))
+
+    other_core = {"gauss": here + 1 - 2 * core, "view": view}
+
+    def over_views(action):
+        for step in (2, 1, 3):
+            other = lax.rem(view + step, VIEWS)
+            action(step, other, {"gauss": here, "view": other})
 
     barrier = pltpu.get_barrier_semaphore()
 
-    def greet(step, other, device):
+    def greet(device):
         pl.semaphore_signal(barrier, inc=1, device_id=device, device_id_type=MESH)
 
-    each(on_line, LINE, greet)
-    each(in_group, GROUP, greet)
-    each(over_views, VIEWS, greet)
-
-    def swap_blocks(peers, count, mine, source, target_buffer, sent, arrived):
-        def copy(step, other, device):
-            return pltpu.make_async_remote_copy(
-                src_ref=source.at[other],
-                dst_ref=target_buffer.at[mine],
-                send_sem=sent.at[step],
-                recv_sem=arrived.at[mine],
-                device_id=device,
-                device_id_type=MESH,
-            )
-
-        def wait(step, other, device):
-            pltpu.make_async_remote_copy(
-                src_ref=source.at[other],
-                dst_ref=target_buffer.at[other],
-                send_sem=sent.at[step],
-                recv_sem=arrived.at[other],
-                device_id=device,
-                device_id_type=MESH,
-            ).wait()
-
-        each(peers, count, lambda *peer: copy(*peer).start())
-        target_buffer[mine] = source[mine]
-        return lambda: each(peers, count, wait)
-
-    table[...] = sender_table(rows[...])
+    far_first(lambda other, device: greet(device))
+    over_views(lambda step, other, device: greet(device))
+    greet(other_core)
+
+    pairs = [
+        (rows_in, rows),
+        (params_in, params),
+        (camera_in, camera),
+        (lists_in, lists),
+        (counts_in, counts),
+        (tile_ids_in, tile_ids),
+        (target_in, target),
+        (first_in, first),
+        (second_in, second),
+    ]
+    copies = [
+        pltpu.make_async_copy(source, place, loads.at[n]) for n, (source, place) in enumerate(pairs)
+    ]
+    for copy in copies:
+        copy.start()
+
+    def remote(source, place, sent, arrived, device):
+        return pltpu.make_async_remote_copy(
+            src_ref=source,
+            dst_ref=place,
+            send_sem=sent,
+            recv_sem=arrived,
+            device_id=device,
+            device_id_type=MESH,
+        )
+
+    def to_chips(source, place, sent, arrived):
+        def send(other, device):
+            remote(source.at[other], place.at[chip], sent, arrived, device).start()
+
+        far_first(send)
+        place[chip] = source[chip]
+
+    def from_chips(place, arrived):
+        whole = place.at[pl.ds(0, CHIPS - 1)]
+        pltpu.make_async_copy(whole, whole, arrived).wait()
+
+    low_lanes = iota((64, 128), 1) < 64
+    mine = low_lanes == (core == 0)
+
+    def with_other_core(source, place, sent, arrived):
+        copy = remote(source, place, sent, arrived, other_core)
+        copy.start()
+        copy.wait()
+        kept = source[...].reshape(64, 128)
+        return jnp.where(mine, kept, swap(place[...].reshape(64, 128)))
+
+    copies[0].wait()
+    table[...] = sender_table(rows[0])
+    copies[1].wait()
+    copies[2].wait()
     scalars = [camera[0, n] for n in range(12)]
     attributes = project([params[n : n + 1, :] for n in range(59)], scalars)
     messages = pack_messages(
         jnp.concatenate(attributes + [jnp.zeros((7, 512), f32)], axis=0), table[...]
     )
-    msg[...] = messages.reshape(LINE, 4, 128)
-
-    pl.semaphore_wait(barrier, LINE + GROUP + VIEWS - 3)
-    arrive = swap_blocks(on_line, LINE, line, msg, land1, send1, recv1)
+    msg[...] = messages.reshape(CHIPS, 1, 128)
+    for copy in copies[3:]:
+        copy.wait()
+
+    pl.semaphore_wait(barrier, CHIPS + VIEWS - 1)
+    to_chips(msg, land1, send1, recv1)
     picked, lane_group = list_tables(lists[0])
-    arrive()
-    low_lanes = iota((8, 128), 1) < 64
-    for pair in range(4):
-        lower, upper = land1[0:8, pair, :], land1[8:16, pair, :]
-        pass1[2 * pair] = jnp.where(low_lanes, lower, swap(upper))
-        pass1[2 * pair + 1] = jnp.where(low_lanes, swap(lower), upper)
-    arrive = swap_blocks(in_group, GROUP, group, pass1, land2, send2, recv2)
-    arrive()
-
-    found = pick(land2[...].reshape(64, 128), picked, lane_group)
+    from_chips(land1, recv1)
+    received = with_other_core(land1, land2, send2, recv2)
+
+    found = pick(received, picked, lane_group)
     pixel_x, pixel_y = pixels()
     centres = []
     for tile in range(2):
@@ -478,7 +516,7 @@
     carry = lax.fori_loop(0, 32, forward, [fresh, fresh], unroll=4)
     around = []
     for tile in range(2):
-        around.append(between(carry[tile][0], carry[tile][1], target[0, tile]))
+        around.append(between(carry[tile][0], carry[tile][1], target[:, tile, :]))
     spot = iota((1, 128), 1)
     loss[...] = jnp.where(spot == 0, around[0][3], jnp.where(spot == 1, around[1][3], 0.0))
 
@@ -507,61 +545,58 @@
         sums = moments(alphas[tile], weights[tile], around[tile][2])
         grads.append(finish_tile(sums, *centres[tile]))
     grads = jnp.concatenate(grads, axis=1)
-    back1[...] = unpick(grads, picked, lane_group).reshape(GROUP, 8, 128)
-
-    arrive = swap_blocks(in_group, GROUP, group, back1, land3, send3, recv3)
-    arrive()
-    for pair in range(4):
-        even, odd = land3[2 * pair], land3[2 * pair + 1]
-        pass2[0:8, pair, :] = jnp.where(low_lanes, even, swap(odd))
-        pass2[8:16, pair, :] = jnp.where(low_lanes, swap(even), odd)
-    arrive = swap_blocks(on_line, LINE, line, pass2, land4, send4, recv4)
-    arrive()
+    back1[...] = unpick(grads, picked, lane_group)
+
+    back2[...] = with_other_core(back1, land3, send3, recv3).reshape(CHIPS, 1, 128)
+    to_chips(back2, land4, send4, recv4)
+    from_chips(land4, recv4)
     returned = unpack_messages(land4[...].reshape(64, 128), table[...])
 
-    lanes = iota((1, 512), 1)
-    pose = jnp.zeros((1, 512), f32)
+    lanes = iota((1, 128), 1)
+    pose = jnp.zeros((1, 128), f32)
     for n in range(12):
         pose = jnp.where(lanes == n, scalars[n], pose)
-    own[...] = jnp.concatenate([returned[0:9], pose, jnp.zeros((6, 512), f32)], axis=0)
+    for part in range(4):
+        own[10 * part : 10 * part + 9, :] = returned[0:9, 128 * part : 128 * part + 128]
+        own[10 * part + 9 : 10 * part + 10, :] = pose
 
     def share(step, other, device):
-        return pltpu.make_async_remote_copy(
-            src_ref=own,
-            dst_ref=land5.at[view],
-            send_sem=send5.at[step],
-            recv_sem=recv5.at[view],
-            device_id=device,
-            device_id_type=MESH,
-        )
+        remote(own, land5.at[view], send5.at[step], recv5.at[view], device).start()
 
     def take(step, other, device):
-        pltpu.make_async_remote_copy(
-            src_ref=own,
-            dst_ref=land5.at[other],
-            send_sem=send5.at[step],
-            recv_sem=recv5.at[other],
-            device_id=device,
-            device_id_type=MESH,
-        ).wait()
-
-    each(over_views, VIEWS, lambda *peer: share(*peer).start())
+        remote(own, land5.at[other], send5.at[step], recv5.at[other], device).wait()
+
+    over_views(share)
     land5[view] = own[...]
-    each(over_views, VIEWS, take)
+    over_views(take)
     out[...] = land5[...]
 
-
-def update(params, first, second, grads, loss, new_params, new_first, new_second, tile_loss, whole):
-    columns = [jnp.broadcast_to(params[n : n + 1, :], (VIEWS, 512)) for n in range(59)]
-    camera = [grads[:, 9, n : n + 1] for n in range(12)]
-    attributes, back = jax.vjp(lambda rows: project(rows, camera)[0:5] + project(rows, camera)[6:9], columns)
-    given = [grads[:, n, :] for n in range(9)]
-    pulled = back(given[0:5] + given[6:9])[0]
-    opacity = 1.0 / (1.0 + jnp.exp(-columns[10]))
-    pulled[10] = given[5] * (1.0 - opacity)
+    for sent, buffer in ((send1, msg), (send4, back2)):
+        whole = buffer.at[pl.ds(0, CHIPS - 1)]
+        pltpu.make_async_copy(whole, whole, sent).wait()
+
+
+def update(
+    params, first, second, grads, loss, new_params, new_first, new_second, tile_loss, spread, total
+):
+    for part in range(4):
+        block = params[:, 128 * part : 128 * part + 128]
+        for view in range(VIEWS):
+            start = 64 * (4 * view + part)
+            spread[start : start + 59, :] = block
+    columns = [spread[pl.ds(n, 16, stride=64), :] for n in range(59)]
+    given = [grads[pl.ds(n, 16, stride=10), :] for n in range(10)]
+    camera = [given[9][:, n : n + 1] for n in range(12)]
+
+    def shown(rows):
+        attributes = project(rows, camera)
+        return attributes[0:5] + attributes[6:9]
+
+    pulled = jax.vjp(shown, columns)[1](given[0:5] + given[6:9])[0]
+    pulled[10] = given[5] * (1.0 - 1.0 / (1.0 + jnp.exp(-columns[10])))
     for n in range(59):
-        whole[n : n + 1, :] = jnp.sum(pulled[n], axis=0, keepdims=True)
-    total = whole[...]
+        both = pulled[n][0:8] + pulled[n][8:16]
+        total[pl.ds(n, 4, stride=64), :] = both[0:4] + both[4:8]
     row = iota((59, 1), 0)
     rate = jnp.where(row < 3, 0.00016, 0.005)
     rate = jnp.where(row < 6, rate, 0.001)
@@ -569,51 +604,65 @@
     rate = jnp.where(row < 11, rate, 0.0025)
     rate = jnp.where(row < 14, rate, 0.000125)
     rate = rate / (1.0 - beta_one**adam_step)
-    moved = beta_one * first[...] + (1.0 - beta_one) * total
-    spread = beta_two * second[...] + (1.0 - beta_two) * total * total
-    new_first[...] = moved
-    new_second[...] = spread
-    new_params[...] = params[...] - rate * moved / (
-        jnp.sqrt(spread / (1.0 - beta_two**adam_step)) + adam_eps
-    )
+    for part in range(4):
+        here = slice(128 * part, 128 * part + 128)
+        slope = total[64 * part : 64 * part + 59, :]
+        moved = beta_one * first[:, here] + (1.0 - beta_one) * slope
+        square = beta_two * second[:, here] + (1.0 - beta_two) * slope * slope
+        new_first[:, here] = moved
+        new_second[:, here] = square
+        new_params[:, here] = params[:, here] - rate * moved / (
+            jnp.sqrt(square / (1.0 - beta_two**adam_step)) + adam_eps
+        )
     tile_loss[...] = loss[:, 0:2]
 
 
 def body(params, first_moment, second_moment, cameras, send_rows, lists, counts, tile_ids, target):
     vmem = pl.BlockSpec(memory_space=pltpu.VMEM)
-    smem = pl.BlockSpec(memory_space=pltpu.SMEM)
+    hbm = pl.BlockSpec(memory_space=pltpu.HBM)
     dma = pltpu.SemaphoreType.DMA
-    grads, loss = pl.pallas_call(
+    whole = jax.ShapeDtypeStruct((59, 512), f32)
+    messages = pltpu.VMEM((CHIPS, 1, 128), f32)
+    params_near, first_near, second_near, grads, loss = pl.pallas_call(
         exchange,
         out_shape=(
-            jax.ShapeDtypeStruct((VIEWS, 16, 512), f32),
+            whole,
+            whole,
+            whole,
+            jax.ShapeDtypeStruct((VIEWS, 40, 128), f32),
             jax.ShapeDtypeStruct((1, 128), f32),
         ),
-        in_specs=[vmem, smem, vmem, vmem, smem, smem, vmem],
-        out_specs=(vmem, vmem),
+        in_specs=[hbm] * 9,
+        out_specs=(vmem,) * 5,
         scratch_shapes=[
-            pltpu.VMEM((LINE, 4, 128), f32),
-            pltpu.VMEM((LINE, 4, 128), f32),
-            pltpu.VMEM((GROUP, 8, 128), f32),
-            pltpu.VMEM((GROUP, 8, 128), f32),
-            pltpu.VMEM((GROUP, 8, 128), f32),
-            pltpu.VMEM((GROUP, 8, 128), f32),
-            pltpu.VMEM((LINE, 4, 128), f32),
-            pltpu.VMEM((LINE, 4, 128), f32),
-            pltpu.VMEM((16, 512), f32),
-            pltpu.VMEM((VIEWS, 16, 512), f32),
+            pltpu.SMEM((1, 12), f32),
+            pltpu.VMEM((1, 1, 512), jnp.int32),
+            pltpu.VMEM((1, 2, 256), jnp.int32),
+            pltpu.SMEM((1, 2), jnp.int32),
+            pltpu.SMEM((1, 2), jnp.int32),
+            pltpu.VMEM((3, 2, 256), f32),
+            messages,
+            messages,
+            messages,
+            pltpu.VMEM((CHIPS, 128), f32),
+            pltpu.VMEM((CHIPS, 128), f32),
+            messages,
+            messages,
+            pltpu.VMEM((40, 128), f32),
+            pltpu.VMEM((VIEWS, 40, 128), f32),
             pltpu.VMEM((2, 256, 128), f32),
             pltpu.VMEM((2, 256, 256), f32),
             pltpu.VMEM((2, 256, 256), f32),
             pltpu.VMEM((512, 512), bf16),
-            dma((LINE,)),
-            dma((LINE,)),
-            dma((GROUP,)),
-            dma((GROUP,)),
-            dma((GROUP,)),
-            dma((GROUP,)),
-            dma((LINE,)),
-            dma((LINE,)),
+            dma((9,)),
+            dma,
+            dma,
+            dma,
+            dma,
+            dma,
+            dma,
+            dma,
+            dma,
             dma((VIEWS,)),
             dma((VIEWS,)),
         ],
@@ -621,17 +670,26 @@
             collective_id=0, has_side_effects=True, vmem_limit_bytes=32 * 1024 * 1024
         ),
         name="exchange",
-    )(params, cameras, send_rows.reshape(1, 512), lists, counts, tile_ids, target)
-    whole = jax.ShapeDtypeStruct((59, 512), f32)
+    )(
+        params,
+        first_moment,
+        second_moment,
+        cameras,
+        send_rows,
+        lists,
+        counts,
+        tile_ids,
+        target[0].transpose(1, 0, 2),
+    )
     return pl.pallas_call(
         update,
         out_shape=(whole, whole, whole, jax.ShapeDtypeStruct((1, 2), f32)),
         in_specs=[vmem] * 5,
         out_specs=(vmem,) * 4,
-        scratch_shapes=[pltpu.VMEM((59, 512), f32)],
+        scratch_shapes=[pltpu.VMEM((1024, 128), f32), pltpu.VMEM((256, 128), f32)],
         compiler_params=pltpu.CompilerParams(vmem_limit_bytes=32 * 1024 * 1024),
         name="update",
-    )(params, first_moment, second_moment, grads, loss)
+    )(params_near, first_near, second_near, grads.reshape(VIEWS * 40, 128), loss)
 
 
 def solution(mesh):

time: 55.3 us -> 52.2 us (0.944)
  Pallas kernels: 51.8 us -> 45.8 us
  local copies, waits for them, and re-layouts: 2.55 us -> 5.43 us
    pallas_call x1, Pallas kernels: 50.2 us -> 44.5 us  [body(): pl.pallas_call(exchange, out_shape=(whole, whole, whole, jax.ShapeDtypeSt...]
    unnamed x17 -> x18, local copies, waits for them, and re-layouts: 2.55 us -> 5.43 us
where the time goes in v2:
time: 52.2 us; the launch traced here: 51.9 us
  Pallas kernels  45.8 us (88%)
  local copies, waits for them, and re-layouts  5.43 us (10%)
  between operations  0.67 us (1%)
    pallas_call x1, Pallas kernels, body(): pl.pallas_call(exchange, out_shape=(whole, whole, whole, jax.ShapeDtypeSt...  44.5 us
    unnamed x18, local copies, waits for them, and re-layouts  5.43 us
    pallas_call x1, Pallas kernels, body(): pl.pallas_call(update, out_shape=(whole, whole, whole, jax.ShapeDtypeStru...  1.37 us

profile of v2, /device:TPU:1, one launch (start us, length us, event | category | flops | bytes accessed | tf_op | source)
XLA Modules:
  0.0 51.9 jit_solution(7782059279810164783)
XLA Ops:
  0.6 0.0 copy-start.8
  0.6 0.0 copy-start.7
  0.7 0.0 copy-start.6
  0.7 0.6 %copy-done.8 = s32[1,2]{1,0:T(1,128)S(1)} copy-done((s32[1,2]{1,0:T(1,128)S(1)}, s32[1,2]{1,0:T(1,128)}, u32[]{:S(2)}) %copy-start.8) | copy-done | bytes 32
  1.3 0.0 copy-done.7
  1.3 0.0 copy-done.6
  1.3 0.0 copy-start
  1.3 0.9 %copy-done = f32[59,512]{1,0:T(8,128)S(1)} copy-done((f32[59,512]{1,0:T(8,128)S(1)}, f32[59,512]{1,0:T(8,128)}, u32[]{:S(2)}) %copy-start) | copy-done | bytes 120856
  2.2 0.0 copy-start.1
  2.2 0.9 %copy-done.1 = f32[59,512]{1,0:T(8,128)S(1)} copy-done((f32[59,512]{1,0:T(8,128)S(1)}, f32[59,512]{1,0:T(8,128)}, u32[]{:S(2)}) %copy-start.1) | copy-done | bytes 120856
  3.1 0.0 copy-start.2
  3.1 0.9 %copy-done.2 = f32[59,512]{1,0:T(8,128)S(1)} copy-done((f32[59,512]{1,0:T(8,128)S(1)}, f32[59,512]{1,0:T(8,128)}, u32[]{:S(2)}) %copy-start.2) | copy-done | bytes 120856
  4.0 0.0 copy-start.3
  4.0 0.7 %copy-done.3 = f32[1,2,3,256]{3,1,2,0:T(2,128)S(1)} copy-done((f32[1,2,3,256]{3,1,2,0:T(2,128)S(1)}, f32[1,2,3,256]{3,1,2,0:T(2,128)}, u32[]{:S(2)}) %copy-start.3) | copy-done | bytes 6168
  4.7 0.0 copy-start.4
  4.7 0.7 %copy-done.4 = s32[1,1,512]{2,1,0:T(1,128)S(1)} copy-done((s32[1,1,512]{2,1,0:T(1,128)S(1)}, s32[1,1,512]{2,1,0:T(1,128)}, u32[]{:S(2)}) %copy-start.4) | copy-done | bytes 2072
  5.4 0.0 copy-start.5
  5.4 0.7 %copy-done.5 = s32[1,2,256]{2,1,0:T(2,128)S(1)} copy-done((s32[1,2,256]{2,1,0:T(2,128)S(1)}, s32[1,2,256]{2,1,0:T(2,128)}, u32[]{:S(2)}) %copy-start.5) | copy-done | bytes 2072
  6.1 44.5 %exchange.1 = (f32[59,512]{1,0:T(8,128)S(1)}, f32[59,512]{1,0:T(8,128)S(1)}, f32[59,512]{1,0:T(8,128)S(1)}, f32[4,40,128]{2,1,0:T(8,128)S(1)}, f32[1,128]{1,0:T(1,128)S(1)}) custom-call(f32[59,512]{1,0:T(8,128)S(1)} %copy-done, f32[59,512]{1,0:T(8,128)S(1)} %copy-done.1, f32[59,512]{1,0:T(8,128)S(1)} %copy-done.2, f32[1,12]{1,0:T(1,128)S(1)} %copy-done.6, ...), custom_call_target="tpu_custom_call" | custom-call | tf_op jit(solution)/shard_map/exchange/pallas_call | solution.py:626
  50.6 1.4 %update.1 = (f32[59,512]{1,0:T(8,128)}, f32[59,512]{1,0:T(8,128)}, f32[59,512]{1,0:T(8,128)}, f32[1,2]{1,0:T(1,128)}) custom-call(f32[59,512]{1,0:T(8,128)S(1)} %get-tuple-element.9.params, f32[59,512]{1,0:T(8,128)S(1)} %get-tuple-element.10.first, f32[59,512]{1,0:T(8,128)S(1)} %get-tuple-element.11.second, f32[160,128]{1,0:T(8,128)S(1)} %bitcast.4, ...), custom_call_target="tpu_custom_call" | custom-call | tf_op jit(solution)/shard_map/update/pallas_call | solution.py:684
Async XLA Ops:
  0.6 0.7 %copy-start.8 = (s32[1,2]{1,0:T(1,128)S(1)}, s32[1,2]{1,0:T(1,128)}, u32[]{:S(2)}) copy-start(s32[1,2]{1,0:T(1,128)} %tile_ids_in.1) | copy-start | bytes 28
  0.6 0.7 %copy-start.7 = (s32[1,2]{1,0:T(1,128)S(1)}, s32[1,2]{1,0:T(1,128)}, u32[]{:S(2)}) copy-start(s32[1,2]{1,0:T(1,128)} %counts_in.1) | copy-start | bytes 28
  0.7 0.7 %copy-start.6 = (f32[1,12]{1,0:T(1,128)S(1)}, f32[1,12]{1,0:T(1,128)}, u32[]{:S(2)}) copy-start(f32[1,12]{1,0:T(1,128)} %camera_in.1) | copy-start | bytes 148
  1.3 0.9 %copy-start = (f32[59,512]{1,0:T(8,128)S(1)}, f32[59,512]{1,0:T(8,128)}, u32[]{:S(2)}) copy-start(f32[59,512]{1,0:T(8,128)} %params_in.1) | copy-start | bytes 362500
  2.2 0.9 %copy-start.1 = (f32[59,512]{1,0:T(8,128)S(1)}, f32[59,512]{1,0:T(8,128)}, u32[]{:S(2)}) copy-start(f32[59,512]{1,0:T(8,128)} %first_in.1) | copy-start | bytes 362500
  3.1 0.9 %copy-start.2 = (f32[59,512]{1,0:T(8,128)S(1)}, f32[59,512]{1,0:T(8,128)}, u32[]{:S(2)}) copy-start(f32[59,512]{1,0:T(8,128)} %second_in.1) | copy-start | bytes 362500
  4.0 0.7 %copy-start.3 = (f32[1,2,3,256]{3,1,2,0:T(2,128)S(1)}, f32[1,2,3,256]{3,1,2,0:T(2,128)}, u32[]{:S(2)}) copy-start(f32[1,2,3,256]{3,1,2,0:T(2,128)} %param.17) | copy-start | bytes 18436
  4.7 0.7 %copy-start.4 = (s32[1,1,512]{2,1,0:T(1,128)S(1)}, s32[1,1,512]{2,1,0:T(1,128)}, u32[]{:S(2)}) copy-start(s32[1,1,512]{2,1,0:T(1,128)} %rows_in.1) | copy-start | bytes 6148
  5.4 0.7 %copy-start.5 = (s32[1,2,256]{2,1,0:T(2,128)S(1)}, s32[1,2,256]{2,1,0:T(2,128)}, u32[]{:S(2)}) copy-start(s32[1,2,256]{2,1,0:T(2,128)} %lists_in.1) | copy-start | bytes 6148

commit v3 on v2

--- a/solution.py
+++ b/solution.py
@@ -35,6 +35,7 @@
 SIDE = 4
 CHIPS = LINE * SIDE
 VIEWS = 4
+VMEM_BYTES = 62 * 1024 * 1024
 MESH = pl.DeviceIdType.MESH
 f32 = jnp.float32
 bf16 = jnp.bfloat16
@@ -342,19 +343,15 @@
 
 def exchange(
     params_in,
-    first_in,
-    second_in,
     camera_in,
     rows_in,
     lists_in,
     counts_in,
     tile_ids_in,
     target_in,
-    params,
-    first,
-    second,
     out,
     loss,
+    params,
     camera,
     rows,
     lists,
@@ -369,7 +366,7 @@
     back2,
     land4,
     own,
-    land5,
+    losses,
     columns,
     alphas,
     weights,
@@ -385,6 +382,7 @@
     recv4,
     send5,
     recv5,
+    kept5,
 ):
     here = lax.axis_index("gauss")
     view = lax.axis_index("view")
@@ -432,8 +430,6 @@
         (counts_in, counts),
         (tile_ids_in, tile_ids),
         (target_in, target),
-        (first_in, first),
-        (second_in, second),
     ]
     copies = [
         pltpu.make_async_copy(source, place, loads.at[n]) for n, (source, place) in enumerate(pairs)
@@ -518,7 +514,9 @@
     for tile in range(2):
         around.append(between(carry[tile][0], carry[tile][1], target[:, tile, :]))
     spot = iota((1, 128), 1)
-    loss[...] = jnp.where(spot == 0, around[0][3], jnp.where(spot == 1, around[1][3], 0.0))
+    losses[...] = jnp.where(spot == 0, around[0][3], jnp.where(spot == 1, around[1][3], 0.0))
+    loss_copy = pltpu.make_async_copy(losses, loss, loads.at[7])
+    loss_copy.start()
 
     def backward(step, later):
         rows_here = pl.ds(pl.multiple_of((31 - step) * 8, 8), 8)
@@ -561,30 +559,63 @@
         own[10 * part + 9 : 10 * part + 10, :] = pose
 
     def share(step, other, device):
-        remote(own, land5.at[view], send5.at[step], recv5.at[view], device).start()
+        remote(own, out.at[view], send5.at[step], recv5.at[view], device).start()
 
     def take(step, other, device):
-        remote(own, land5.at[other], send5.at[step], recv5.at[other], device).wait()
+        remote(own, out.at[other], send5.at[step], recv5.at[other], device).wait()
 
     over_views(share)
-    land5[view] = own[...]
-    over_views(take)
-    out[...] = land5[...]
+    keep = pltpu.make_async_copy(own, out.at[view], kept5)
+    keep.start()
+    loss_copy.wait()
 
     for sent, buffer in ((send1, msg), (send4, back2)):
         whole = buffer.at[pl.ds(0, CHIPS - 1)]
         pltpu.make_async_copy(whole, whole, sent).wait()
+    keep.wait()
+    over_views(take)
 
 
 def update(
-    params, first, second, grads, loss, new_params, new_first, new_second, tile_loss, spread, total
+    params_in,
+    first_in,
+    second_in,
+    grads_in,
+    loss_in,
+    new_params,
+    new_first,
+    new_second,
+    tile_loss,
+    params,
+    first,
+    second,
+    grads,
+    loss,
+    spread,
+    total,
+    loads,
 ):
+    pairs = [
+        (params_in, params),
+        (grads_in, grads),
+        (first_in, first),
+        (second_in, second),
+        (loss_in, loss),
+    ]
+    copies = [
+        pltpu.make_async_copy(source, place, loads.at[n]) for n, (source, place) in enumerate(pairs)
+    ]
+    for copy in copies:
+        copy.start()
+    copies[0].wait()
+
     for part in range(4):
         block = params[:, 128 * part : 128 * part + 128]
         for view in range(VIEWS):
             start = 64 * (4 * view + part)
             spread[start : start + 59, :] = block
     columns = [spread[pl.ds(n, 16, stride=64), :] for n in range(59)]
+    copies[1].wait()
     given = [grads[pl.ds(n, 16, stride=10), :] for n in range(10)]
     camera = [given[9][:, n : n + 1] for n in range(12)]
 
@@ -597,6 +628,8 @@
     for n in range(59):
         both = pulled[n][0:8] + pulled[n][8:16]
         total[pl.ds(n, 4, stride=64), :] = both[0:4] + both[4:8]
+    for copy in copies[2:]:
+        copy.wait()
     row = iota((59, 1), 0)
     rate = jnp.where(row < 3, 0.00016, 0.005)
     rate = jnp.where(row < 6, rate, 0.001)
@@ -623,18 +656,17 @@
     dma = pltpu.SemaphoreType.DMA
     whole = jax.ShapeDtypeStruct((59, 512), f32)
     messages = pltpu.VMEM((CHIPS, 1, 128), f32)
-    params_near, first_near, second_near, grads, loss = pl.pallas_call(
+    some = pltpu.CompilerParams(vmem_limit_bytes=VMEM_BYTES)
+    grads, loss = pl.pallas_call(
         exchange,
         out_shape=(
-            whole,
-            whole,
-            whole,
             jax.ShapeDtypeStruct((VIEWS, 40, 128), f32),
             jax.ShapeDtypeStruct((1, 128), f32),
         ),
-        in_specs=[hbm] * 9,
-        out_specs=(vmem,) * 5,
+        in_specs=[hbm] * 7,
+        out_specs=(hbm,) * 2,
         scratch_shapes=[
+            pltpu.VMEM((59, 512), f32),
             pltpu.SMEM((1, 12), f32),
             pltpu.VMEM((1, 1, 512), jnp.int32),
             pltpu.VMEM((1, 2, 256), jnp.int32),
@@ -649,12 +681,12 @@
             messages,
             messages,
             pltpu.VMEM((40, 128), f32),
-            pltpu.VMEM((VIEWS, 40, 128), f32),
+            pltpu.VMEM((1, 128), f32),
             pltpu.VMEM((2, 256, 128), f32),
             pltpu.VMEM((2, 256, 256), f32),
             pltpu.VMEM((2, 256, 256), f32),
             pltpu.VMEM((512, 512), bf16),
-            dma((9,)),
+            dma((8,)),
             dma,
             dma,
             dma,
@@ -665,15 +697,14 @@
             dma,
             dma((VIEWS,)),
             dma((VIEWS,)),
+            dma,
         ],
         compiler_params=pltpu.CompilerParams(
-            collective_id=0, has_side_effects=True, vmem_limit_bytes=32 * 1024 * 1024
+            collective_id=0, has_side_effects=True, vmem_limit_bytes=VMEM_BYTES
         ),
         name="exchange",
     )(
         params,
-        first_moment,
-        second_moment,
         cameras,
         send_rows,
         lists,
@@ -681,15 +712,25 @@
         tile_ids,
         target[0].transpose(1, 0, 2),
     )
+    near = pltpu.VMEM((59, 512), f32)
     return pl.pallas_call(
         update,
         out_shape=(whole, whole, whole, jax.ShapeDtypeStruct((1, 2), f32)),
-        in_specs=[vmem] * 5,
+        in_specs=[hbm] * 5,
         out_specs=(vmem,) * 4,
-        scratch_shapes=[pltpu.VMEM((1024, 128), f32), pltpu.VMEM((256, 128), f32)],
-        compiler_params=pltpu.CompilerParams(vmem_limit_bytes=32 * 1024 * 1024),
+        scratch_shapes=[
+            near,
+            near,
+            near,
+            pltpu.VMEM((VIEWS * 40, 128), f32),
+            pltpu.VMEM((1, 128), f32),
+            pltpu.VMEM((1024, 128), f32),
+            pltpu.VMEM((256, 128), f32),
+            dma((5,)),
+        ],
+        compiler_params=some,
         name="update",
-    )(params_near, first_near, second_near, grads.reshape(VIEWS * 40, 128), loss)
+    )(params, first_moment, second_moment, grads.reshape(VIEWS * 40, 128), loss)
 
 
 def solution(mesh):

time: 52.2 us -> 47.7 us (0.914)
  local copies, waits for them, and re-layouts: 5.43 us -> 0 us
  Pallas kernels: 45.8 us -> 46.9 us
    unnamed x18 -> x0, local copies, waits for them, and re-layouts: 5.43 us -> none
    pallas_call x1, Pallas kernels: 1.37 us -> 2.39 us  [body(): pl.pallas_call(update, out_shape=(whole, whole, whole, jax.ShapeDtypeStru...]
where the time goes in v3:
time: 47.7 us; the launch traced here: 47.6 us
  Pallas kernels  46.9 us (98%)
  between operations  0.64 us (1%)
    pallas_call x1, Pallas kernels, body(): pl.pallas_call(exchange, out_shape=(jax.ShapeDtypeStruct((VIEWS, 40, 128)...  44.6 us
    pallas_call x1, Pallas kernels, body(): pl.pallas_call(update, out_shape=(whole, whole, whole, jax.ShapeDtypeStru...  2.39 us

profile of v3, /device:TPU:1, one launch (start us, length us, event | category | flops | bytes accessed | tf_op | source)
XLA Modules:
  0.0 47.6 jit_solution(7530496104527637726)
XLA Ops:
  0.6 44.6 %exchange.1 = (f32[4,40,128]{2,1,0:T(8,128)}, f32[1,128]{1,0:T(1,128)}) custom-call(f32[59,512]{1,0:T(8,128)} %params_in.3, f32[1,12]{1,0:T(1,128)} %camera_in.1, s32[1,1,512]{2,1,0:T(1,128)} %rows_in.1, s32[1,2,256]{2,1,0:T(2,128)} %lists_in.1, s32[1,2]{1,0:T(1,128)} %counts_in.1, s32[1,2]{1,0:T(1,128)} %tile_ids_in.1, f32[3,2,256]{2,1,0:T(2,128)} %bitcast.5), custom_call_target="tpu_custom_call" | custom-call | tf_op jit(solution)/shard_map/exchange/pallas_call | solution.py:660
  45.2 2.4 %update.1 = (f32[59,512]{1,0:T(8,128)}, f32[59,512]{1,0:T(8,128)}, f32[59,512]{1,0:T(8,128)}, f32[1,2]{1,0:T(1,128)}) custom-call(f32[59,512]{1,0:T(8,128)} %params_in.3, f32[59,512]{1,0:T(8,128)} %first_in.1, f32[59,512]{1,0:T(8,128)} %second_in.1, f32[160,128]{1,0:T(8,128)} %bitcast.4, f32[1,128]{1,0:T(1,128)} %get-tuple-element.7.loss_in), custom_call_target="tpu_custom_call" | custom-call | tf_op jit(solution)/shard_map/update/pallas_call | solution.py:716

commit v4 on v3

--- a/solution.py
+++ b/solution.py
@@ -237,24 +237,27 @@
     return 32 * (position & 7) + (position >> 3)
 
 
+def split(rows):
+    return [part.astype(f32) for part in pieces(rows)]
+
+
 def prepare_tile(attributes, count, tile_id):
     across = (16 * lax.rem(tile_id, 120)).astype(f32) + 7.5
     down = (16 * lax.div(tile_id, 120)).astype(f32) + 7.5
     centre_u = attributes[0:1] - across
     centre_v = attributes[1:2] - down
     alive = place_of(iota((1, 256), 1)) < count
-    rows = [
-        centre_u,
-        centre_v,
-        attributes[2:3] * (-0.5 * log2_e),
-        attributes[3:4] * (-log2_e),
-        attributes[4:5] * (-0.5 * log2_e),
-        jnp.where(alive, attributes[5:6], 0.0),
-        attributes[6:7],
-        attributes[7:8],
-        attributes[8:9],
-        jnp.zeros((119, 256), f32),
-    ]
+    by_xx = attributes[2:3] * (-0.5 * log2_e)
+    by_xy = attributes[3:4] * (-log2_e)
+    by_yy = attributes[4:5] * (-0.5 * log2_e)
+    by_x = -2.0 * by_xx * centre_u - by_xy * centre_v
+    by_y = -2.0 * by_yy * centre_v - by_xy * centre_u
+    whole = (by_xx * centre_u + by_xy * centre_v) * centre_u + (by_yy * centre_v) * centre_v
+    whole = jnp.where(alive, whole + jnp.log(attributes[5:6]) * log2_e, -1e30)
+    power = split(jnp.concatenate([whole, by_x, by_y, by_xx, by_xy, by_yy], axis=0))
+    colour = attributes[6:9]
+    high, middle, low = split(colour)
+    rows = power + [high, high, high, middle, middle, low, colour, jnp.zeros((89, 256), f32)]
     return jnp.transpose(jnp.concatenate(rows, axis=0)), centre_u, centre_v
 
 
@@ -263,17 +266,30 @@
     return (number & 15).astype(f32) - 7.5, (number >> 4).astype(f32) - 7.5
 
 
-def shade_step(columns, pixel_x, pixel_y, carry):
+def monomials():
+    pixel_x, pixel_y = pixels()
+    ones = jnp.ones((1, 256), f32)
+    return [ones, pixel_x, pixel_y, pixel_x * pixel_x, pixel_x * pixel_y, pixel_y * pixel_y]
+
+
+def exponents(columns):
+    right = jnp.concatenate(monomials() * 3 + [jnp.zeros((110, 256), f32)], axis=0)
+    return jnp.dot(columns, right.astype(bf16), preferred_element_type=f32)
+
+
+def shades(columns, residual):
+    high, middle, low = split(jnp.concatenate(residual, axis=0))
+    rows = [jnp.zeros((18, 256), f32), high, middle, low, high, middle, high]
+    right = jnp.concatenate(rows + [jnp.zeros((92, 256), f32)], axis=0)
+    return jnp.dot(columns, right.astype(bf16), preferred_element_type=f32)
+
+
+def shade_step(columns, power, carry):
     keep, colour = carry
-    offset_x = pixel_x - columns[:, 0:1]
-    offset_y = pixel_y - columns[:, 1:2]
-    power = offset_x * (columns[:, 2:3] * offset_x + columns[:, 3:4] * offset_y) + (
-        columns[:, 4:5] * offset_y
-    ) * offset_y
-    alpha = columns[:, 5:6] * jnp.exp2(power)
+    alpha = jnp.exp2(power)
     weight = keep * alpha
-    colour = [colour[c] + weight * columns[:, 6 + c : 7 + c] for c in range(3)]
-    return alpha, weight, (keep * (1.0 - alpha), colour)
+    colour = [colour[c] + weight * columns[:, 36 + c : 37 + c] for c in range(3)]
+    return alpha, weight, (keep - weight, colour)
 
 
 def between(keep, colour, target):
@@ -292,27 +308,22 @@
     return before, after, residual, 0.5 * jnp.sum(squares, axis=1, keepdims=True)
 
 
-def back_step(columns, alpha, weight, before, after, residual, later):
-    shade = (
-        residual[0] * columns[:, 6:7] + residual[1] * columns[:, 7:8] + residual[2] * columns[:, 8:9]
-    )
+def back_step(shade, alpha, weight, before, after, later):
     own = weight * shade
     left = 1.0 - alpha
     guess = pl.reciprocal(left, approx=True)
     ratio = alpha * (guess * (2.0 - left * guess))
-    slope = before * (own - later * ratio) - after * ratio
+    slope = before * own - (before * later + after) * ratio
     return slope, before * weight, later + own
 
 
 def moments(slope, weight, residual):
-    pixel_x, pixel_y = pixels()
-    ones = jnp.ones((1, 256), f32)
-    powers = [ones, pixel_x, pixel_y, pixel_x * pixel_x, pixel_x * pixel_y, pixel_y * pixel_y]
-    shown = [part.astype(f32) for part in pieces(jnp.concatenate(residual, axis=0))]
-    factors = jnp.concatenate(powers + shown + [jnp.zeros((1, 256), f32)], axis=0).astype(bf16)
+    shown = split(jnp.concatenate(residual, axis=0))
+    factors = jnp.concatenate(monomials() + shown + [jnp.zeros((1, 256), f32)], axis=0).astype(bf16)
 
     def over_pixels(value):
-        return sum(dot_rows(factors, part) for part in pieces(value)[::-1])
+        high, middle, unused = pieces(value)
+        return dot_rows(factors, middle) + dot_rows(factors, high)
 
     by_power = over_pixels(slope)[0:6]
     by_shown = over_pixels(weight)
@@ -370,6 +381,7 @@
     columns,
     alphas,
     weights,
+    shaded,
     table,
     loads,
     send1,
@@ -488,12 +500,12 @@
     received = with_other_core(land1, land2, send2, recv2)
 
     found = pick(received, picked, lane_group)
-    pixel_x, pixel_y = pixels()
     centres = []
     for tile in range(2):
         entries = found[:, 256 * tile : 256 * tile + 256]
         filled, centre_u, centre_v = prepare_tile(entries, counts[0, tile], tile_ids[0, tile])
         columns[tile] = filled
+        alphas[tile] = exponents(filled.astype(bf16))
         centres.append((entries, centre_u, centre_v))
 
     def forward(step, carry):
@@ -501,7 +513,7 @@
         left = []
         for tile in range(2):
             alpha, weight, rest = shade_step(
-                columns[tile, rows_here, :], pixel_x, pixel_y, carry[tile]
+                columns[tile, rows_here, :], alphas[tile, rows_here, :], carry[tile]
             )
             alphas[tile, rows_here, :] = alpha
             weights[tile, rows_here, :] = weight
@@ -509,10 +521,11 @@
         return left
 
     fresh = (jnp.ones((8, 256), f32), [jnp.zeros((8, 256), f32)] * 3)
-    carry = lax.fori_loop(0, 32, forward, [fresh, fresh], unroll=4)
+    carry = lax.fori_loop(0, 32, forward, [fresh, fresh], unroll=16)
     around = []
     for tile in range(2):
         around.append(between(carry[tile][0], carry[tile][1], target[:, tile, :]))
+        shaded[tile] = shades(columns[tile].astype(bf16), around[tile][2])
     spot = iota((1, 128), 1)
     losses[...] = jnp.where(spot == 0, around[0][3], jnp.where(spot == 1, around[1][3], 0.0))
     loss_copy = pltpu.make_async_copy(losses, loss, loads.at[7])
@@ -522,14 +535,13 @@
         rows_here = pl.ds(pl.multiple_of((31 - step) * 8, 8), 8)
         left = []
         for tile in range(2):
-            before, after, residual, unused = around[tile]
+            before, after = around[tile][0:2]
             slope, weight, rest = back_step(
-                columns[tile, rows_here, :],
+                shaded[tile, rows_here, :],
                 alphas[tile, rows_here, :],
                 weights[tile, rows_here, :],
                 before,
                 after,
-                residual,
                 later[tile],
             )
             alphas[tile, rows_here, :] = slope
@@ -537,7 +549,7 @@
             left.append(rest)
         return left
 
-    lax.fori_loop(0, 32, backward, [jnp.zeros((8, 256), f32)] * 2, unroll=4)
+    lax.fori_loop(0, 32, backward, [jnp.zeros((8, 256), f32)] * 2, unroll=16)
     grads = []
     for tile in range(2):
         sums = moments(alphas[tile], weights[tile], around[tile][2])
@@ -685,6 +697,7 @@
             pltpu.VMEM((2, 256, 128), f32),
             pltpu.VMEM((2, 256, 256), f32),
             pltpu.VMEM((2, 256, 256), f32),
+            pltpu.VMEM((2, 256, 256), f32),
             pltpu.VMEM((512, 512), bf16),
             dma((8,)),
             dma,

time: 47.7 us -> 46.1 us (0.966)
  Pallas kernels: 46.9 us -> 45.4 us
    pallas_call x1, Pallas kernels: 44.6 us -> 43 us  [body(): pl.pallas_call(exchange, out_shape=(jax.ShapeDtypeStruct((VIEWS, 40, 128)...]
where the time goes in v4:
time: 46.1 us; the launch traced here: 46 us
  Pallas kernels  45.4 us (98%)
  between operations  0.64 us (1%)
    pallas_call x1, Pallas kernels, body(): pl.pallas_call(exchange, out_shape=(jax.ShapeDtypeStruct((VIEWS, 40, 128)...  43 us
    pallas_call x1, Pallas kernels, body(): pl.pallas_call(update, out_shape=(whole, whole, whole, jax.ShapeDtypeStru...  2.39 us

profile of v4, /device:TPU:1, one launch (start us, length us, event | category | flops | bytes accessed | tf_op | source)
XLA Modules:
  0.0 46.0 jit_solution(3595275680468312689)
XLA Ops:
  0.6 43.0 %exchange.1 = (f32[4,40,128]{2,1,0:T(8,128)}, f32[1,128]{1,0:T(1,128)}) custom-call(f32[59,512]{1,0:T(8,128)} %params_in.3, f32[1,12]{1,0:T(1,128)} %camera_in.1, s32[1,1,512]{2,1,0:T(1,128)} %rows_in.1, s32[1,2,256]{2,1,0:T(2,128)} %lists_in.1, s32[1,2]{1,0:T(1,128)} %counts_in.1, s32[1,2]{1,0:T(1,128)} %tile_ids_in.1, f32[3,2,256]{2,1,0:T(2,128)} %bitcast.5), custom_call_target="tpu_custom_call" | custom-call | tf_op jit(solution)/shard_map/exchange/pallas_call | solution.py:672
  43.6 2.4 %update.1 = (f32[59,512]{1,0:T(8,128)}, f32[59,512]{1,0:T(8,128)}, f32[59,512]{1,0:T(8,128)}, f32[1,2]{1,0:T(1,128)}) custom-call(f32[59,512]{1,0:T(8,128)} %params_in.3, f32[59,512]{1,0:T(8,128)} %first_in.1, f32[59,512]{1,0:T(8,128)} %second_in.1, f32[160,128]{1,0:T(8,128)} %bitcast.4, f32[1,128]{1,0:T(1,128)} %get-tuple-element.7.loss_in), custom_call_target="tpu_custom_call" | custom-call | tf_op jit(solution)/shard_map/update/pallas_call | solution.py:729

commit v5 on v4

--- a/solution.py
+++ b/solution.py
@@ -34,6 +34,8 @@
 LINE = 16
 SIDE = 4
 CHIPS = LINE * SIDE
+SHARE = 4
+RENDER = CHIPS // SHARE
 VIEWS = 4
 VMEM_BYTES = 62 * 1024 * 1024
 MESH = pl.DeviceIdType.MESH
@@ -176,16 +178,18 @@
     return pltpu.roll(value, 64, 1)
 
 
-def reorder_row(row, width, place):
-    split = jnp.concatenate([row >> 4, row & 15, jnp.zeros((6, width), jnp.int32)], axis=0)
+def reorder_rows(rows, place):
+    number, width = rows.shape
+    padding = jnp.zeros((8 - 2 * number, width), jnp.int32)
+    split_rows = jnp.concatenate([rows >> 4, rows & 15, padding], axis=0)
     chosen = one_hot(iota((width, width), 0) == place(iota((width, width), 1)))
-    moved = jnp.dot(split.astype(f32).astype(bf16), chosen, preferred_element_type=f32)
-    return (moved[0:1] * 16.0 + moved[1:2]).astype(jnp.int32)
+    moved = jnp.dot(split_rows.astype(f32).astype(bf16), chosen, preferred_element_type=f32)
+    return moved[0:number] * 16.0 + moved[number : 2 * number]
 
 
 def sender_table(rows):
-    moved = reorder_row(rows, 512, lambda n: 8 * (n & 63) + (n >> 6))
-    return one_hot(iota((512, 512), 0) == moved)
+    moved = reorder_rows(rows, lambda n: 8 * (n & 63) + (n >> 6))
+    return one_hot(iota((512, 512), 0) == moved.astype(jnp.int32))
 
 
 def pack_messages(attributes, table):
@@ -209,10 +213,7 @@
 
 
 def list_tables(lists):
-    moved = []
-    for tile in range(2):
-        moved.append(reorder_row(lists[tile : tile + 1], 256, lambda n: 32 * (n & 7) + (n >> 3)))
-    slot = jnp.concatenate(moved, axis=1)
+    slot = jnp.concatenate([lists[0:1], lists[1:2]], axis=1).astype(jnp.int32)
     return one_hot(iota((64, 512), 0) == (slot >> 3)), slot & 7
 
 
@@ -241,12 +242,28 @@
     return [part.astype(f32) for part in pieces(rows)]
 
 
-def prepare_tile(attributes, count, tile_id):
-    across = (16 * lax.rem(tile_id, 120)).astype(f32) + 7.5
-    down = (16 * lax.div(tile_id, 120)).astype(f32) + 7.5
+def split(rows):
+    return [part.astype(f32) for part in pieces(rows)]
+
+
+def two_pieces(value):
+    high = value.astype(bf16)
+    return high, (value - high.astype(f32)).astype(bf16)
+
+
+def padded(rows):
+    number = sum(part.shape[0] for part in rows)
+    return jnp.concatenate(rows + [jnp.zeros((32 - number, 256), f32)], axis=0).astype(bf16)
+
+
+def dot_columns(left, right):
+    return lax.dot_general(left, right, (((0,), (0,)), ((), ())), preferred_element_type=f32)
+
+
+def prepare_tile(attributes, across, down, count):
     centre_u = attributes[0:1] - across
     centre_v = attributes[1:2] - down
-    alive = place_of(iota((1, 256), 1)) < count
+    alive = place_of(iota((1, 256), 1)).astype(f32) < count
     by_xx = attributes[2:3] * (-0.5 * log2_e)
     by_xy = attributes[3:4] * (-log2_e)
     by_yy = attributes[4:5] * (-0.5 * log2_e)
@@ -254,11 +271,8 @@
     by_y = -2.0 * by_yy * centre_v - by_xy * centre_u
     whole = (by_xx * centre_u + by_xy * centre_v) * centre_u + (by_yy * centre_v) * centre_v
     whole = jnp.where(alive, whole + jnp.log(attributes[5:6]) * log2_e, -1e30)
-    power = split(jnp.concatenate([whole, by_x, by_y, by_xx, by_xy, by_yy], axis=0))
-    colour = attributes[6:9]
-    high, middle, low = split(colour)
-    rows = power + [high, high, high, middle, middle, low, colour, jnp.zeros((89, 256), f32)]
-    return jnp.transpose(jnp.concatenate(rows, axis=0)), centre_u, centre_v
+    power = jnp.concatenate([whole, by_x, by_y, by_xx, by_xy, by_yy], axis=0)
+    return power, centre_u, centre_v
 
 
 def pixels():
@@ -272,24 +286,26 @@
     return [ones, pixel_x, pixel_y, pixel_x * pixel_x, pixel_x * pixel_y, pixel_y * pixel_y]
 
 
-def exponents(columns):
-    right = jnp.concatenate(monomials() * 3 + [jnp.zeros((110, 256), f32)], axis=0)
-    return jnp.dot(columns, right.astype(bf16), preferred_element_type=f32)
-
-
-def shades(columns, residual):
+def exponents(power):
+    return dot_columns(padded(split(power)), padded(monomials() * 3))
+
+
+def colour_sums(colour, weight):
+    chunk = (iota((8, 256), 1) & 7) == iota((8, 256), 0)
+    spread = [jnp.where(chunk, colour[c : c + 1], 0.0) for c in range(3)]
+    left = jnp.concatenate(split(jnp.concatenate(spread, axis=0)), axis=0).astype(bf16)
+    high, middle = two_pieces(weight)
+    total = jnp.dot(left, middle, preferred_element_type=f32)
+    total = total + jnp.dot(left, high, preferred_element_type=f32)
+    total = add_pieces(total)
+    return [total[8 * c : 8 * c + 8] for c in range(3)]
+
+
+def shades(colour, residual):
+    high, middle, low = split(colour)
+    left = padded([high, high, high, middle, middle, low])
     high, middle, low = split(jnp.concatenate(residual, axis=0))
-    rows = [jnp.zeros((18, 256), f32), high, middle, low, high, middle, high]
-    right = jnp.concatenate(rows + [jnp.zeros((92, 256), f32)], axis=0)
-    return jnp.dot(columns, right.astype(bf16), preferred_element_type=f32)
-
-
-def shade_step(columns, power, carry):
-    keep, colour = carry
-    alpha = jnp.exp2(power)
-    weight = keep * alpha
-    colour = [colour[c] + weight * columns[:, 36 + c : 37 + c] for c in range(3)]
-    return alpha, weight, (keep - weight, colour)
+    return dot_columns(left, padded([high, middle, low, high, middle, high]))
 
 
 def between(keep, colour, target):
@@ -322,7 +338,7 @@
     factors = jnp.concatenate(monomials() + shown + [jnp.zeros((1, 256), f32)], axis=0).astype(bf16)
 
     def over_pixels(value):
-        high, middle, unused = pieces(value)
+        high, middle = two_pieces(value)
         return dot_rows(factors, middle) + dot_rows(factors, high)
 
     by_power = over_pixels(slope)[0:6]
@@ -376,9 +392,11 @@
     land3,
     back2,
     land4,
+    facts,
+    land_facts,
     own,
     losses,
-    columns,
+    away,
     alphas,
     weights,
     shaded,
@@ -395,6 +413,10 @@
     send5,
     recv5,
     kept5,
+    send6,
+    recv6,
+    send7,
+    recv7,
 ):
     here = lax.axis_index("gauss")
     view = lax.axis_index("view")
@@ -403,21 +425,6 @@
     line = chip // SIDE
     side = lax.rem(chip, SIDE)
 
-    def on_chip(step_z, step_x):
-        other = lax.rem(line + step_z, LINE) * SIDE + lax.rem(side + step_x, SIDE)
-        return other, {"gauss": other * 2 + core, "view": view}
-
-    def far_first(action):
-        def one(step, unused):
-            step_z = LINE // 2 + (1 - 2 * (step & 1)) * ((step + 1) >> 1)
-            for step_x in (2, 1, 3, 0):
-                action(*on_chip(step_z, step_x))
-            return unused
-
-        lax.fori_loop(0, LINE - 1, one, 0)
-        for step_x in (2, 1, 3):
-            action(*on_chip(0, step_x))
-
     other_core = {"gauss": here + 1 - 2 * core, "view": view}
 
     def over_views(action):
@@ -430,9 +437,40 @@
     def greet(device):
         pl.semaphore_signal(barrier, inc=1, device_id=device, device_id_type=MESH)
 
-    far_first(lambda other, device: greet(device))
+    early = chip < RENDER
+    late = jnp.logical_not(early)
+    home = {"gauss": lax.rem(chip, RENDER) * 2 + core, "view": view}
+    turn = chip // RENDER
+
+    def served(number):
+        return {"gauss": lax.rem(chip + number * RENDER, CHIPS) * 2 + core, "view": view}
+
+    def to_renderers(action):
+        for step_z in (0, 1, 3, 2):
+            for step_x in (2, 1, 3, 0):
+                other = lax.rem(line + step_z, 4) * SIDE + lax.rem(side + step_x, SIDE)
+                device = {"gauss": other * 2 + core, "view": view}
+                pl.when(other != chip)(lambda other=other, device=device: action(other, device))
+
+    def to_all(action):
+        def one(number, unused):
+            for step_x in (2, 1, 3, 0):
+                other = number * SIDE + lax.rem(side + step_x, SIDE)
+                device = {"gauss": other * 2 + core, "view": view}
+                pl.when(other != chip)(lambda other=other, device=device: action(other, device))
+            return unused
+
+        lax.fori_loop(0, LINE, one, 0)
+
+    def greet_late(other, device):
+        pl.when(other >= RENDER)(lambda: greet(device))
+
+    @pl.when(early)
+    def greet_first():
+        to_renderers(lambda other, device: greet(device))
+        greet(other_core)
+
     over_views(lambda step, other, device: greet(device))
-    greet(other_core)
 
     pairs = [
         (rows_in, rows),
@@ -448,6 +486,8 @@
     ]
     for copy in copies:
         copy.start()
+
+    pl.when(early)(lambda: to_all(greet_late))
 
     def remote(source, place, sent, arrived, device):
         return pltpu.make_async_remote_copy(
@@ -459,16 +499,9 @@
             device_id_type=MESH,
         )
 
-    def to_chips(source, place, sent, arrived):
-        def send(other, device):
-            remote(source.at[other], place.at[chip], sent, arrived, device).start()
-
-        far_first(send)
-        place[chip] = source[chip]
-
-    def from_chips(place, arrived):
-        whole = place.at[pl.ds(0, CHIPS - 1)]
-        pltpu.make_async_copy(whole, whole, arrived).wait()
+    def wait_rows(place, count, semaphore):
+        whole = place.at[pl.ds(0, count)]
+        pltpu.make_async_copy(whole, whole, semaphore).wait()
 
     low_lanes = iota((64, 128), 1) < 64
     mine = low_lanes == (core == 0)
@@ -477,8 +510,9 @@
         copy = remote(source, place, sent, arrived, other_core)
         copy.start()
         copy.wait()
-        kept = source[...].reshape(64, 128)
-        return jnp.where(mine, kept, swap(place[...].reshape(64, 128)))
+
+    def joined(kept, given):
+        return jnp.where(mine, kept, swap(given))
 
     copies[0].wait()
     table[...] = sender_table(rows[0])
@@ -489,78 +523,145 @@
     messages = pack_messages(
         jnp.concatenate(attributes + [jnp.zeros((7, 512), f32)], axis=0), table[...]
     )
-    msg[...] = messages.reshape(CHIPS, 1, 128)
+    for number in range(SHARE):
+        msg[:, number, :] = messages[RENDER * number : RENDER * number + RENDER]
     for copy in copies[3:]:
         copy.wait()
 
-    pl.semaphore_wait(barrier, CHIPS + VIEWS - 1)
-    to_chips(msg, land1, send1, recv1)
-    picked, lane_group = list_tables(lists[0])
-    from_chips(land1, recv1)
-    received = with_other_core(land1, land2, send2, recv2)
-
-    found = pick(received, picked, lane_group)
-    centres = []
+    facts[0:2, :] = reorder_rows(lists[0], place_of)
     for tile in range(2):
-        entries = found[:, 256 * tile : 256 * tile + 256]
-        filled, centre_u, centre_v = prepare_tile(entries, counts[0, tile], tile_ids[0, tile])
-        columns[tile] = filled
-        alphas[tile] = exponents(filled.astype(bf16))
-        centres.append((entries, centre_u, centre_v))
-
-    def forward(step, carry):
-        rows_here = pl.ds(pl.multiple_of(step * 8, 8), 8)
-        left = []
-        for tile in range(2):
-            alpha, weight, rest = shade_step(
-                columns[tile, rows_here, :], alphas[tile, rows_here, :], carry[tile]
-            )
-            alphas[tile, rows_here, :] = alpha
-            weights[tile, rows_here, :] = weight
-            left.append(rest)
-        return left
-
-    fresh = (jnp.ones((8, 256), f32), [jnp.zeros((8, 256), f32)] * 3)
-    carry = lax.fori_loop(0, 32, forward, [fresh, fresh], unroll=16)
-    around = []
+        for channel in range(3):
+            row = 2 + 3 * tile + channel
+            facts[row : row + 1, :] = target[channel, tile : tile + 1, :]
+    spots = iota((1, 256), 1)
+    known = jnp.zeros((1, 256), f32)
     for tile in range(2):
-        around.append(between(carry[tile][0], carry[tile][1], target[:, tile, :]))
-        shaded[tile] = shades(columns[tile].astype(bf16), around[tile][2])
-    spot = iota((1, 128), 1)
-    losses[...] = jnp.where(spot == 0, around[0][3], jnp.where(spot == 1, around[1][3], 0.0))
+        tile_id = tile_ids[0, tile]
+        across = (16 * lax.rem(tile_id, 120)).astype(f32) + 7.5
+        down = (16 * lax.div(tile_id, 120)).astype(f32) + 7.5
+        for n, value in enumerate((across, down, counts[0, tile].astype(f32))):
+            known = jnp.where(spots == 3 * tile + n, value, known)
+    facts[8:16, :] = jnp.concatenate([known, jnp.zeros((7, 256), f32)], axis=0)
+
+    pl.semaphore_wait(barrier, RENDER + VIEWS - 1)
+
+    def send_attributes(other, device):
+        remote(msg.at[other], land1.at[chip], send1, recv1, device).start()
+
+    def send_gradients(other, device):
+        remote(back2.at[other], land4.at[chip], send4, recv4, device).start()
+
+    @pl.when(late)
+    def send_facts():
+        remote(facts, land_facts.at[turn - 1], send6, recv6.at[turn - 1], home).start()
+
+    to_renderers(send_attributes)
+
+    @pl.when(late)
+    def late_part():
+        remote(facts, land_facts.at[turn - 1], send6, recv6.at[turn - 1], home).wait_send()
+        wait_rows(msg, RENDER, send1)
+        remote(away.at[0], losses, send7.at[0], recv7, home).wait_recv()
+        wait_rows(land4, RENDER, recv4)
+
+    @pl.when(early)
+    def render():
+        land1[chip] = msg[chip]
+        tables = [list_tables(facts[0:2, :])]
+        for number in range(1, SHARE):
+            place = land_facts.at[number - 1]
+            remote(facts, place, send6, recv6.at[number - 1], served(number)).wait_recv()
+            tables.append(list_tables(land_facts[number - 1, 0:2, :]))
+        wait_rows(land1, CHIPS - 1, recv1)
+        with_other_core(land1, land2, send2, recv2)
+
+        tiles = range(2 * SHARE)
+        entries, centres, shown = [], [], []
+        for number in range(SHARE):
+            found = pick(joined(land1[:, number, :], land2[:, number, :]), *tables[number])
+            known = facts[...] if number == 0 else land_facts[number - 1]
+            for part in range(2):
+                chosen = found[:, 256 * part : 256 * part + 256]
+                about = [known[8:9, 3 * part + n : 3 * part + n + 1] for n in range(3)]
+                power, centre_u, centre_v = prepare_tile(chosen, *about)
+                alphas[2 * number + part] = exponents(power)
+                entries.append(chosen)
+                centres.append((centre_u, centre_v))
+                shown.append(known[2 + 3 * part : 5 + 3 * part])
+
+        def forward(step, carry):
+            rows_here = pl.ds(pl.multiple_of(step * 8, 8), 8)
+            left = []
+            for tile, keep in zip(tiles, carry):
+                alpha = jnp.exp2(alphas[tile, rows_here, :])
+                weight = keep * alpha
+                alphas[tile, rows_here, :] = alpha
+                weights[tile, rows_here, :] = weight
+                left.append(keep - weight)
+            return left
+
+        keeps = lax.fori_loop(0, 32, forward, [jnp.ones((8, 256), f32) for tile in tiles], unroll=4)
+        around = []
+        for tile in tiles:
+            colour = colour_sums(entries[tile][6:9], weights[tile])
+            around.append(between(keeps[tile], colour, shown[tile]))
+            shaded[tile] = shades(entries[tile][6:9], around[tile][2])
+        spot = iota((1, 128), 1)
+        for number in range(SHARE):
+            pair = around[2 * number][3], around[2 * number + 1][3]
+            row = jnp.where(spot == 0, pair[0], jnp.where(spot == 1, pair[1], 0.0))
+            if number == 0:
+                losses[...] = row
+            else:
+                away[number - 1] = row
+                place = away.at[number - 1]
+                remote(place, losses, send7.at[number - 1], recv7, served(number)).start()
+
+        for first_tile in range(0, 2 * SHARE, 4):
+            some = range(first_tile, first_tile + 4)
+
+            def backward(step, later, some=some):
+                rows_here = pl.ds(pl.multiple_of((31 - step) * 8, 8), 8)
+                left = []
+                for tile, behind in zip(some, later):
+                    before, after = around[tile][0:2]
+                    slope, weight, rest = back_step(
+                        shaded[tile, rows_here, :],
+                        alphas[tile, rows_here, :],
+                        weights[tile, rows_here, :],
+                        before,
+                        after,
+                        behind,
+                    )
+                    alphas[tile, rows_here, :] = slope
+                    weights[tile, rows_here, :] = weight
+                    left.append(rest)
+                return left
+
+            lax.fori_loop(0, 32, backward, [jnp.zeros((8, 256), f32)] * 4, unroll=8)
+        for number in range(SHARE):
+            grads = []
+            for tile in (2 * number, 2 * number + 1):
+                sums = moments(alphas[tile], weights[tile], around[tile][2])
+                grads.append(finish_tile(sums, entries[tile], *centres[tile]))
+            back1[number] = unpick(jnp.concatenate(grads, axis=1), *tables[number])
+
+        with_other_core(back1, land3, send3, recv3)
+        for number in range(SHARE):
+            back2[:, number, :] = joined(back1[number], land3[number])
+        to_all(send_gradients)
+        land4[chip] = back2[chip]
+        for number in range(1, SHARE):
+            place = away.at[number - 1]
+            remote(place, losses, send7.at[number - 1], recv7, served(number)).wait_send()
+        wait_rows(msg, RENDER - 1, send1)
+        wait_rows(land4, RENDER - 1, recv4)
+
     loss_copy = pltpu.make_async_copy(losses, loss, loads.at[7])
     loss_copy.start()
-
-    def backward(step, later):
-        rows_here = pl.ds(pl.multiple_of((31 - step) * 8, 8), 8)
-        left = []
-        for tile in range(2):
-            before, after = around[tile][0:2]
-            slope, weight, rest = back_step(
-                shaded[tile, rows_here, :],
-                alphas[tile, rows_here, :],
-                weights[tile, rows_here, :],
-                before,
-                after,
-                later[tile],
-            )
-            alphas[tile, rows_here, :] = slope
-            weights[tile, rows_here, :] = weight
-            left.append(rest)
-        return left
-
-    lax.fori_loop(0, 32, backward, [jnp.zeros((8, 256), f32)] * 2, unroll=16)
-    grads = []
-    for tile in range(2):
-        sums = moments(alphas[tile], weights[tile], around[tile][2])
-        grads.append(finish_tile(sums, *centres[tile]))
-    grads = jnp.concatenate(grads, axis=1)
-    back1[...] = unpick(grads, picked, lane_group)
-
-    back2[...] = with_other_core(back1, land3, send3, recv3).reshape(CHIPS, 1, 128)
-    to_chips(back2, land4, send4, recv4)
-    from_chips(land4, recv4)
-    returned = unpack_messages(land4[...].reshape(64, 128), table[...])
+    returned = unpack_messages(
+        jnp.concatenate([land4[:, number, :] for number in range(SHARE)], axis=0), table[...]
+    )
 
     lanes = iota((1, 128), 1)
     pose = jnp.zeros((1, 128), f32)
@@ -579,11 +680,8 @@
     over_views(share)
     keep = pltpu.make_async_copy(own, out.at[view], kept5)
     keep.start()
+    pl.when(early)(lambda: wait_rows(back2, CHIPS - 1, send4))
     loss_copy.wait()
-
-    for sent, buffer in ((send1, msg), (send4, back2)):
-        whole = buffer.at[pl.ds(0, CHIPS - 1)]
-        pltpu.make_async_copy(whole, whole, sent).wait()
     keep.wait()
     over_views(take)
 
@@ -667,7 +765,6 @@
     hbm = pl.BlockSpec(memory_space=pltpu.HBM)
     dma = pltpu.SemaphoreType.DMA
     whole = jax.ShapeDtypeStruct((59, 512), f32)
-    messages = pltpu.VMEM((CHIPS, 1, 128), f32)
     some = pltpu.CompilerParams(vmem_limit_bytes=VMEM_BYTES)
     grads, loss = pl.pallas_call(
         exchange,
@@ -685,19 +782,21 @@
             pltpu.SMEM((1, 2), jnp.int32),
             pltpu.SMEM((1, 2), jnp.int32),
             pltpu.VMEM((3, 2, 256), f32),
-            messages,
-            messages,
-            messages,
-            pltpu.VMEM((CHIPS, 128), f32),
-            pltpu.VMEM((CHIPS, 128), f32),
-            messages,
-            messages,
+            pltpu.VMEM((RENDER, SHARE, 128), f32),
+            pltpu.VMEM((CHIPS, SHARE, 128), f32),
+            pltpu.VMEM((CHIPS, SHARE, 128), f32),
+            pltpu.VMEM((SHARE, CHIPS, 128), f32),
+            pltpu.VMEM((SHARE, CHIPS, 128), f32),
+            pltpu.VMEM((CHIPS, SHARE, 128), f32),
+            pltpu.VMEM((RENDER, SHARE, 128), f32),
+            pltpu.VMEM((16, 256), f32),
+            pltpu.VMEM((SHARE - 1, 16, 256), f32),
             pltpu.VMEM((40, 128), f32),
             pltpu.VMEM((1, 128), f32),
-            pltpu.VMEM((2, 256, 128), f32),
-            pltpu.VMEM((2, 256, 256), f32),
-            pltpu.VMEM((2, 256, 256), f32),
-            pltpu.VMEM((2, 256, 256), f32),
+            pltpu.VMEM((SHARE - 1, 1, 128), f32),
+            pltpu.VMEM((2 * SHARE, 256, 256), f32),
+            pltpu.VMEM((2 * SHARE, 256, 256), f32),
+            pltpu.VMEM((2 * SHARE, 256, 256), f32),
             pltpu.VMEM((512, 512), bf16),
             dma((8,)),
             dma,
@@ -710,6 +809,10 @@
             dma,
             dma((VIEWS,)),
             dma((VIEWS,)),
+            dma,
+            dma,
+            dma((SHARE - 1,)),
+            dma((SHARE - 1,)),
             dma,
         ],
         compiler_params=pltpu.CompilerParams(

time: 46.1 us -> 44.4 us (0.963)
  Pallas kernels: 45.4 us -> 43.6 us
    pallas_call x1, Pallas kernels: 43 us -> 41.2 us  [body(): pl.pallas_call(exchange, out_shape=(jax.ShapeDtypeStruct((VIEWS, 40, 128)...]
where the time goes in v5:
time: 44.4 us; the launch traced here: 44.2 us
  Pallas kernels  43.6 us (98%)
  between operations  0.64 us (1%)
    pallas_call x1, Pallas kernels, body(): pl.pallas_call(exchange, out_shape=(jax.ShapeDtypeStruct((VIEWS, 40, 128)...  41.2 us
    pallas_call x1, Pallas kernels, body(): pl.pallas_call(update, out_shape=(whole, whole, whole, jax.ShapeDtypeStru...  2.39 us

profile of v5, /device:TPU:1, one launch (start us, length us, event | category | flops | bytes accessed | tf_op | source)
XLA Modules:
  0.0 44.2 jit_solution(13527902296889665204)
XLA Ops:
  0.6 41.2 %exchange.1 = (f32[4,40,128]{2,1,0:T(8,128)}, f32[1,128]{1,0:T(1,128)}) custom-call(f32[59,512]{1,0:T(8,128)} %params_in.3, f32[1,12]{1,0:T(1,128)} %camera_in.1, s32[1,1,512]{2,1,0:T(1,128)} %rows_in.1, s32[1,2,256]{2,1,0:T(2,128)} %lists_in.1, s32[1,2]{1,0:T(1,128)} %counts_in.1, s32[1,2]{1,0:T(1,128)} %tile_ids_in.1, f32[3,2,256]{2,1,0:T(2,128)} %bitcast.5), custom_call_target="tpu_custom_call" | custom-call | tf_op jit(solution)/shard_map/exchange/pallas_call | solution.py:769
  41.8 2.4 %update.1 = (f32[59,512]{1,0:T(8,128)}, f32[59,512]{1,0:T(8,128)}, f32[59,512]{1,0:T(8,128)}, f32[1,2]{1,0:T(1,128)}) custom-call(f32[59,512]{1,0:T(8,128)} %params_in.3, f32[59,512]{1,0:T(8,128)} %first_in.1, f32[59,512]{1,0:T(8,128)} %second_in.1, f32[160,128]{1,0:T(8,128)} %bitcast.4, f32[1,128]{1,0:T(1,128)} %get-tuple-element.7.loss_in), custom_call_target="tpu_custom_call" | custom-call | tf_op jit(solution)/shard_map/update/pallas_call | solution.py:832

commit v6 on v5

--- a/solution.py
+++ b/solution.py
@@ -194,11 +194,18 @@
 
 def pack_messages(attributes, table):
     placed = dot_exact(attributes, table)
-    parts = []
-    for pair in range(4):
-        both = placed[:, 128 * pair : 128 * pair + 128]
-        parts += [both, swap(both)]
-    return jnp.transpose(jnp.concatenate(parts, axis=0))[0:64]
+    turned = jnp.transpose(jnp.concatenate([placed, jnp.zeros((112, 512), f32)], axis=0))
+    lanes = iota((16, 128), 1)
+    rows = [jnp.zeros((16, 128), f32)] * 3
+    for group in range(8):
+        for number in range(SHARE):
+            slot = SHARE * group + number
+            block = turned[16 * slot : 16 * slot + 16]
+            most = jnp.where(lanes < 8, block, 0.0)
+            last = jnp.where(lanes == 8, block, 0.0)
+            rows[group // 4] = rows[group // 4] + pltpu.roll(most, 8 * (slot % 16), 1)
+            rows[2] = rows[2] + pltpu.roll(last, (8 * number + group - 8) % 128, 1)
+    return rows
 
 
 def unpack_messages(messages, table):
@@ -217,14 +224,25 @@
     return one_hot(iota((64, 512), 0) == (slot >> 3)), slot & 7
 
 
-def pick(received, table, group):
-    turned = jnp.transpose(jnp.concatenate([received, jnp.zeros_like(received)], axis=0))[:, 0:64]
-    found = dot_exact(turned, table)
-    found = jnp.where((iota((128, 512), 0) >> 4) == group, found, 0.0)
-    total = found[0:16]
+def turn_received(rows):
+    blank = jnp.zeros((64, 128), f32)
+    return [jnp.transpose(jnp.concatenate([row, blank], axis=0))[:, 0:64] for row in rows]
+
+
+def pick(first, second, core, number, table, group):
+    most, last = [], []
+    for turned in (first, second):
+        mine = jnp.where(core == 0, turned[0], turned[1])
+        most += [mine[8 * (SHARE * n + number) :][0:8] for n in range(4)]
+        ninth = turned[2][8 * number : 8 * number + 8]
+        last.append(jnp.where(core == 0, ninth[0:4], ninth[4:8]))
+    found = dot_exact(jnp.concatenate(most + last, axis=0), table)
+    eight = jnp.where((iota((64, 512), 0) >> 3) == group, found[0:64], 0.0)
+    total = eight[0:8]
     for part in range(1, 8):
-        total = total + found[16 * part : 16 * part + 16]
-    return total
+        total = total + eight[8 * part : 8 * part + 8]
+    ninth = jnp.where(iota((8, 512), 0) == group, found[64:72], 0.0)
+    return jnp.concatenate([total, jnp.sum(ninth, axis=0, keepdims=True)], axis=0)
 
 
 def unpick(grads, table, group):
@@ -523,8 +541,8 @@
     messages = pack_messages(
         jnp.concatenate(attributes + [jnp.zeros((7, 512), f32)], axis=0), table[...]
     )
-    for number in range(SHARE):
-        msg[:, number, :] = messages[RENDER * number : RENDER * number + RENDER]
+    for number in range(3):
+        msg[:, number, 0, :] = messages[number]
     for copy in copies[3:]:
         copy.wait()
 
@@ -575,10 +593,14 @@
         wait_rows(land1, CHIPS - 1, recv1)
         with_other_core(land1, land2, send2, recv2)
 
+        kept = turn_received([land1[:, n, 0, :] for n in range(3)])
+        given = turn_received([land2[:, n, 0, :] for n in range(3)])
+        first = [jnp.where(core == 0, a, b) for a, b in zip(kept, given)]
+        second = [jnp.where(core == 0, b, a) for a, b in zip(kept, given)]
         tiles = range(2 * SHARE)
         entries, centres, shown = [], [], []
         for number in range(SHARE):
-            found = pick(joined(land1[:, number, :], land2[:, number, :]), *tables[number])
+            found = pick(first, second, core, number, *tables[number])
             known = facts[...] if number == 0 else land_facts[number - 1]
             for part in range(2):
                 chosen = found[:, 256 * part : 256 * part + 256]
@@ -782,9 +804,9 @@
             pltpu.SMEM((1, 2), jnp.int32),
             pltpu.SMEM((1, 2), jnp.int32),
             pltpu.VMEM((3, 2, 256), f32),
-            pltpu.VMEM((RENDER, SHARE, 128), f32),
-            pltpu.VMEM((CHIPS, SHARE, 128), f32),
-            pltpu.VMEM((CHIPS, SHARE, 128), f32),
+            pltpu.VMEM((RENDER, 3, 1, 128), f32),
+            pltpu.VMEM((CHIPS, 3, 1, 128), f32),
+            pltpu.VMEM((CHIPS, 3, 1, 128), f32),
             pltpu.VMEM((SHARE, CHIPS, 128), f32),
             pltpu.VMEM((SHARE, CHIPS, 128), f32),
             pltpu.VMEM((CHIPS, SHARE, 128), f32),

time: 44.4 us -> 42.6 us (0.959)
  Pallas kernels: 43.6 us -> 41.9 us
    pallas_call x1, Pallas kernels: 41.2 us -> 39.5 us  [body(): pl.pallas_call(exchange, out_shape=(jax.ShapeDtypeStruct((VIEWS, 40, 128)...]
where the time goes in v6:
time: 42.6 us; the launch traced here: 42.5 us
  Pallas kernels  41.9 us (98%)
  between operations  0.64 us (2%)
    pallas_call x1, Pallas kernels, body(): pl.pallas_call(exchange, out_shape=(jax.ShapeDtypeStruct((VIEWS, 40, 128)...  39.5 us
    pallas_call x1, Pallas kernels, body(): pl.pallas_call(update, out_shape=(whole, whole, whole, jax.ShapeDtypeStru...  2.39 us

profile of v6, /device:TPU:1, one launch (start us, length us, event | category | flops | bytes accessed | tf_op | source)
XLA Modules:
  0.0 42.5 jit_solution(3255662216252892987)
XLA Ops:
  0.6 39.5 %exchange.1 = (f32[4,40,128]{2,1,0:T(8,128)}, f32[1,128]{1,0:T(1,128)}) custom-call(f32[59,512]{1,0:T(8,128)} %params_in.3, f32[1,12]{1,0:T(1,128)} %camera_in.1, s32[1,1,512]{2,1,0:T(1,128)} %rows_in.1, s32[1,2,256]{2,1,0:T(2,128)} %lists_in.1, s32[1,2]{1,0:T(1,128)} %counts_in.1, s32[1,2]{1,0:T(1,128)} %tile_ids_in.1, f32[3,2,256]{2,1,0:T(2,128)} %bitcast.5), custom_call_target="tpu_custom_call" | custom-call | tf_op jit(solution)/shard_map/exchange/pallas_call | solution.py:791
  40.1 2.4 %update.1 = (f32[59,512]{1,0:T(8,128)}, f32[59,512]{1,0:T(8,128)}, f32[59,512]{1,0:T(8,128)}, f32[1,2]{1,0:T(1,128)}) custom-call(f32[59,512]{1,0:T(8,128)} %params_in.3, f32[59,512]{1,0:T(8,128)} %first_in.1, f32[59,512]{1,0:T(8,128)} %second_in.1, f32[160,128]{1,0:T(8,128)} %bitcast.4, f32[1,128]{1,0:T(1,128)} %get-tuple-element.7.loss_in), custom_call_target="tpu_custom_call" | custom-call | tf_op jit(solution)/shard_map/update/pallas_call | solution.py:854

commit v7 on v6

--- a/solution.py
+++ b/solution.py
@@ -406,12 +406,12 @@
     msg,
     land1,
     land2,
-    back1,
-    land3,
     back2,
     land4,
     facts,
     land_facts,
+    aims,
+    land_aims,
     own,
     losses,
     away,
@@ -424,8 +424,6 @@
     recv1,
     send2,
     recv2,
-    send3,
-    recv3,
     send4,
     recv4,
     send5,
@@ -435,6 +433,8 @@
     recv6,
     send7,
     recv7,
+    send8,
+    recv8,
 ):
     here = lax.axis_index("gauss")
     view = lax.axis_index("view")
@@ -476,6 +476,20 @@
                 other = number * SIDE + lax.rem(side + step_x, SIDE)
                 device = {"gauss": other * 2 + core, "view": view}
                 pl.when(other != chip)(lambda other=other, device=device: action(other, device))
+            return unused
+
+        lax.fori_loop(0, LINE, one, 0)
+
+    def to_all_cores(action):
+        def one(number, unused):
+            for step_x in (2, 1, 3, 0):
+                other = number * SIDE + lax.rem(side + step_x, SIDE)
+                for which in range(2):
+                    device = {"gauss": other * 2 + which, "view": view}
+                    place = which * CHIPS + other
+                    pl.when(other * 2 + which != here)(
+                        lambda place=place, device=device: action(place, device)
+                    )
             return unused
 
         lax.fori_loop(0, LINE, one, 0)
@@ -521,16 +535,10 @@
         whole = place.at[pl.ds(0, count)]
         pltpu.make_async_copy(whole, whole, semaphore).wait()
 
-    low_lanes = iota((64, 128), 1) < 64
-    mine = low_lanes == (core == 0)
-
     def with_other_core(source, place, sent, arrived):
         copy = remote(source, place, sent, arrived, other_core)
         copy.start()
         copy.wait()
-
-    def joined(kept, given):
-        return jnp.where(mine, kept, swap(given))
 
     copies[0].wait()
     table[...] = sender_table(rows[0])
@@ -546,11 +554,10 @@
     for copy in copies[3:]:
         copy.wait()
 
-    facts[0:2, :] = reorder_rows(lists[0], place_of)
+    facts[0:2, 0, :] = reorder_rows(lists[0], place_of)
     for tile in range(2):
         for channel in range(3):
-            row = 2 + 3 * tile + channel
-            facts[row : row + 1, :] = target[channel, tile : tile + 1, :]
+            aims[3 * tile + channel, 0:1, :] = target[channel, tile : tile + 1, :]
     spots = iota((1, 256), 1)
     known = jnp.zeros((1, 256), f32)
     for tile in range(2):
@@ -559,7 +566,7 @@
         down = (16 * lax.div(tile_id, 120)).astype(f32) + 7.5
         for n, value in enumerate((across, down, counts[0, tile].astype(f32))):
             known = jnp.where(spots == 3 * tile + n, value, known)
-    facts[8:16, :] = jnp.concatenate([known, jnp.zeros((7, 256), f32)], axis=0)
+    facts[2, 0:1, :] = known
 
     pl.semaphore_wait(barrier, RENDER + VIEWS - 1)
 
@@ -567,7 +574,8 @@
         remote(msg.at[other], land1.at[chip], send1, recv1, device).start()
 
     def send_gradients(other, device):
-        remote(back2.at[other], land4.at[chip], send4, recv4, device).start()
+        mine = land4.at[core * RENDER + chip]
+        remote(back2.at[other], mine, send4, recv4, device).start()
 
     @pl.when(late)
     def send_facts():
@@ -577,19 +585,22 @@
 
     @pl.when(late)
     def late_part():
+        aims_copy = remote(aims, land_aims.at[turn - 1], send8, recv8.at[turn - 1], home)
+        aims_copy.start()
         remote(facts, land_facts.at[turn - 1], send6, recv6.at[turn - 1], home).wait_send()
+        aims_copy.wait_send()
         wait_rows(msg, RENDER, send1)
         remote(away.at[0], losses, send7.at[0], recv7, home).wait_recv()
-        wait_rows(land4, RENDER, recv4)
+        wait_rows(land4, 2 * RENDER, recv4)
 
     @pl.when(early)
     def render():
         land1[chip] = msg[chip]
-        tables = [list_tables(facts[0:2, :])]
+        tables = [list_tables(facts[0:2, 0, :])]
         for number in range(1, SHARE):
             place = land_facts.at[number - 1]
             remote(facts, place, send6, recv6.at[number - 1], served(number)).wait_recv()
-            tables.append(list_tables(land_facts[number - 1, 0:2, :]))
+            tables.append(list_tables(land_facts[number - 1, 0:2, 0, :]))
         wait_rows(land1, CHIPS - 1, recv1)
         with_other_core(land1, land2, send2, recv2)
 
@@ -598,18 +609,17 @@
         first = [jnp.where(core == 0, a, b) for a, b in zip(kept, given)]
         second = [jnp.where(core == 0, b, a) for a, b in zip(kept, given)]
         tiles = range(2 * SHARE)
-        entries, centres, shown = [], [], []
+        entries, centres = [], []
         for number in range(SHARE):
             found = pick(first, second, core, number, *tables[number])
-            known = facts[...] if number == 0 else land_facts[number - 1]
+            known = facts[2] if number == 0 else land_facts[number - 1, 2]
             for part in range(2):
                 chosen = found[:, 256 * part : 256 * part + 256]
-                about = [known[8:9, 3 * part + n : 3 * part + n + 1] for n in range(3)]
+                about = [known[:, 3 * part + n : 3 * part + n + 1] for n in range(3)]
                 power, centre_u, centre_v = prepare_tile(chosen, *about)
                 alphas[2 * number + part] = exponents(power)
                 entries.append(chosen)
                 centres.append((centre_u, centre_v))
-                shown.append(known[2 + 3 * part : 5 + 3 * part])
 
         def forward(step, carry):
             rows_here = pl.ds(pl.multiple_of(step * 8, 8), 8)
@@ -623,6 +633,11 @@
             return left
 
         keeps = lax.fori_loop(0, 32, forward, [jnp.ones((8, 256), f32) for tile in tiles], unroll=4)
+        shown = [aims[0:3, 0, :], aims[3:6, 0, :]]
+        for number in range(SHARE - 1):
+            place = land_aims.at[number]
+            remote(aims, place, send8, recv8.at[number], served(number + 1)).wait_recv()
+            shown += [land_aims[number, 0:3, 0, :], land_aims[number, 3:6, 0, :]]
         around = []
         for tile in tiles:
             colour = colour_sums(entries[tile][6:9], weights[tile])
@@ -661,29 +676,36 @@
                 return left
 
             lax.fori_loop(0, 32, backward, [jnp.zeros((8, 256), f32)] * 4, unroll=8)
+        back = []
         for number in range(SHARE):
             grads = []
             for tile in (2 * number, 2 * number + 1):
                 sums = moments(alphas[tile], weights[tile], around[tile][2])
                 grads.append(finish_tile(sums, entries[tile], *centres[tile]))
-            back1[number] = unpick(jnp.concatenate(grads, axis=1), *tables[number])
-
-        with_other_core(back1, land3, send3, recv3)
-        for number in range(SHARE):
-            back2[:, number, :] = joined(back1[number], land3[number])
-        to_all(send_gradients)
-        land4[chip] = back2[chip]
+            back.append(unpick(jnp.concatenate(grads, axis=1), *tables[number]))
+
+        low_lanes = iota((CHIPS, 128), 1) < 64
+        for pair in range(2):
+            one, two = back[2 * pair], back[2 * pair + 1]
+            back2[0:CHIPS, pair, :] = jnp.where(low_lanes, one, swap(two))
+            back2[CHIPS:, pair, :] = jnp.where(low_lanes, swap(one), two)
+        to_all_cores(send_gradients)
+        land4[core * RENDER + chip] = back2[core * CHIPS + chip]
         for number in range(1, SHARE):
             place = away.at[number - 1]
             remote(place, losses, send7.at[number - 1], recv7, served(number)).wait_send()
         wait_rows(msg, RENDER - 1, send1)
-        wait_rows(land4, RENDER - 1, recv4)
+        wait_rows(land4, 2 * RENDER - 1, recv4)
 
     loss_copy = pltpu.make_async_copy(losses, loss, loads.at[7])
     loss_copy.start()
-    returned = unpack_messages(
-        jnp.concatenate([land4[:, number, :] for number in range(SHARE)], axis=0), table[...]
-    )
+    low_rows = iota((RENDER, 128), 1) < 64
+    messages = []
+    for pair in range(2):
+        zero, one = land4[0:RENDER, pair, :], land4[RENDER:, pair, :]
+        messages.append(jnp.where(low_rows, zero, swap(one)))
+        messages.append(jnp.where(low_rows, swap(zero), one))
+    returned = unpack_messages(jnp.concatenate(messages, axis=0), table[...])
 
     lanes = iota((1, 128), 1)
     pose = jnp.zeros((1, 128), f32)
@@ -702,7 +724,7 @@
     over_views(share)
     keep = pltpu.make_async_copy(own, out.at[view], kept5)
     keep.start()
-    pl.when(early)(lambda: wait_rows(back2, CHIPS - 1, send4))
+    pl.when(early)(lambda: wait_rows(back2, 2 * CHIPS - 1, send4))
     loss_copy.wait()
     keep.wait()
     over_views(take)
@@ -807,12 +829,12 @@
             pltpu.VMEM((RENDER, 3, 1, 128), f32),
             pltpu.VMEM((CHIPS, 3, 1, 128), f32),
             pltpu.VMEM((CHIPS, 3, 1, 128), f32),
-            pltpu.VMEM((SHARE, CHIPS, 128), f32),
-            pltpu.VMEM((SHARE, CHIPS, 128), f32),
-            pltpu.VMEM((CHIPS, SHARE, 128), f32),
-            pltpu.VMEM((RENDER, SHARE, 128), f32),
-            pltpu.VMEM((16, 256), f32),
-            pltpu.VMEM((SHARE - 1, 16, 256), f32),
+            pltpu.VMEM((2 * CHIPS, 2, 128), f32),
+            pltpu.VMEM((2 * RENDER, 2, 128), f32),
+            pltpu.VMEM((3, 1, 256), f32),
+            pltpu.VMEM((SHARE - 1, 3, 1, 256), f32),
+            pltpu.VMEM((6, 1, 256), f32),
+            pltpu.VMEM((SHARE - 1, 6, 1, 256), f32),
             pltpu.VMEM((40, 128), f32),
             pltpu.VMEM((1, 128), f32),
             pltpu.VMEM((SHARE - 1, 1, 128), f32),
@@ -827,8 +849,6 @@
             dma,
             dma,
             dma,
-            dma,
-            dma,
             dma((VIEWS,)),
             dma((VIEWS,)),
             dma,
@@ -836,6 +856,8 @@
             dma((SHARE - 1,)),
             dma((SHARE - 1,)),
             dma,
+            dma,
+            dma((SHARE - 1,)),
         ],
         compiler_params=pltpu.CompilerParams(
             collective_id=0, has_side_effects=True, vmem_limit_bytes=VMEM_BYTES

time: 42.6 us -> 42 us (0.986)
  Pallas kernels: 41.9 us -> 41.3 us
    pallas_call x1, Pallas kernels: 39.5 us -> 38.9 us  [body(): pl.pallas_call(exchange, out_shape=(jax.ShapeDtypeStruct((VIEWS, 40, 128)...]
where the time goes in v7:
time: 42 us; the launch traced here: 41.9 us
  Pallas kernels  41.3 us (98%)
  between operations  0.64 us (2%)
    pallas_call x1, Pallas kernels, body(): pl.pallas_call(exchange, out_shape=(jax.ShapeDtypeStruct((VIEWS, 40, 128)...  38.9 us
    pallas_call x1, Pallas kernels, body(): pl.pallas_call(update, out_shape=(whole, whole, whole, jax.ShapeDtypeStru...  2.39 us

profile of v7, /device:TPU:1, one launch (start us, length us, event | category | flops | bytes accessed | tf_op | source)
XLA Modules:
  0.0 41.9 jit_solution(17798375762901141659)
XLA Ops:
  0.6 38.9 %exchange.1 = (f32[4,40,128]{2,1,0:T(8,128)}, f32[1,128]{1,0:T(1,128)}) custom-call(f32[59,512]{1,0:T(8,128)} %params_in.3, f32[1,12]{1,0:T(1,128)} %camera_in.1, s32[1,1,512]{2,1,0:T(1,128)} %rows_in.1, s32[1,2,256]{2,1,0:T(2,128)} %lists_in.1, s32[1,2]{1,0:T(1,128)} %counts_in.1, s32[1,2]{1,0:T(1,128)} %tile_ids_in.1, f32[3,2,256]{2,1,0:T(2,128)} %bitcast.5), custom_call_target="tpu_custom_call" | custom-call | tf_op jit(solution)/shard_map/exchange/pallas_call | solution.py:813
  39.5 2.4 %update.1 = (f32[59,512]{1,0:T(8,128)}, f32[59,512]{1,0:T(8,128)}, f32[59,512]{1,0:T(8,128)}, f32[1,2]{1,0:T(1,128)}) custom-call(f32[59,512]{1,0:T(8,128)} %params_in.3, f32[59,512]{1,0:T(8,128)} %first_in.1, f32[59,512]{1,0:T(8,128)} %second_in.1, f32[160,128]{1,0:T(8,128)} %bitcast.4, f32[1,128]{1,0:T(1,128)} %get-tuple-element.7.loss_in), custom_call_target="tpu_custom_call" | custom-call | tf_op jit(solution)/shard_map/update/pallas_call | solution.py:876

commit v8 on v7

--- a/solution.py
+++ b/solution.py
@@ -229,20 +229,18 @@
     return [jnp.transpose(jnp.concatenate([row, blank], axis=0))[:, 0:64] for row in rows]
 
 
-def pick(first, second, core, number, table, group):
-    most, last = [], []
-    for turned in (first, second):
-        mine = jnp.where(core == 0, turned[0], turned[1])
-        most += [mine[8 * (SHARE * n + number) :][0:8] for n in range(4)]
-        ninth = turned[2][8 * number : 8 * number + 8]
-        last.append(jnp.where(core == 0, ninth[0:4], ninth[4:8]))
-    found = dot_exact(jnp.concatenate(most + last, axis=0), table)
-    eight = jnp.where((iota((64, 512), 0) >> 3) == group, found[0:64], 0.0)
-    total = eight[0:8]
-    for part in range(1, 8):
-        total = total + eight[8 * part : 8 * part + 8]
-    ninth = jnp.where(iota((8, 512), 0) == group, found[64:72], 0.0)
-    return jnp.concatenate([total, jnp.sum(ninth, axis=0, keepdims=True)], axis=0)
+def pick(turned, sender, core, number, table, group):
+    mine = jnp.where(core == 0, turned[0], turned[1])
+    rows = [mine[8 * (SHARE * n + number) :][0:8] for n in range(4)]
+    ninth = turned[2][8 * number : 8 * number + 8]
+    rows.append(jnp.where(core == 0, ninth, pltpu.roll(ninth, 4, 0)))
+    found = dot_exact(jnp.concatenate(rows, axis=0), table)
+    place = group - 4 * sender
+    total = jnp.where(place == 0, found[0:8], 0.0)
+    for part in range(1, 4):
+        total = total + jnp.where(place == part, found[8 * part : 8 * part + 8], 0.0)
+    last = jnp.where(iota((4, 512), 0) == place, found[32:36], 0.0)
+    return jnp.concatenate([total, jnp.sum(last, axis=0, keepdims=True)], axis=0)
 
 
 def unpick(grads, table, group):
@@ -406,6 +404,7 @@
     msg,
     land1,
     land2,
+    halves,
     back2,
     land4,
     facts,
@@ -535,11 +534,6 @@
         whole = place.at[pl.ds(0, count)]
         pltpu.make_async_copy(whole, whole, semaphore).wait()
 
-    def with_other_core(source, place, sent, arrived):
-        copy = remote(source, place, sent, arrived, other_core)
-        copy.start()
-        copy.wait()
-
     copies[0].wait()
     table[...] = sender_table(rows[0])
     copies[1].wait()
@@ -551,6 +545,17 @@
     )
     for number in range(3):
         msg[:, number, 0, :] = messages[number]
+    pl.semaphore_wait(barrier, RENDER + VIEWS - 1)
+
+    def send_attributes(other, device):
+        remote(msg.at[other], land1.at[chip], send1, recv1, device).start()
+
+    def send_gradients(other, device):
+        mine = land4.at[core * RENDER + chip]
+        remote(back2.at[other], mine, send4, recv4, device).start()
+
+    to_renderers(send_attributes)
+
     for copy in copies[3:]:
         copy.wait()
 
@@ -568,20 +573,9 @@
             known = jnp.where(spots == 3 * tile + n, value, known)
     facts[2, 0:1, :] = known
 
-    pl.semaphore_wait(barrier, RENDER + VIEWS - 1)
-
-    def send_attributes(other, device):
-        remote(msg.at[other], land1.at[chip], send1, recv1, device).start()
-
-    def send_gradients(other, device):
-        mine = land4.at[core * RENDER + chip]
-        remote(back2.at[other], mine, send4, recv4, device).start()
-
     @pl.when(late)
     def send_facts():
         remote(facts, land_facts.at[turn - 1], send6, recv6.at[turn - 1], home).start()
-
-    to_renderers(send_attributes)
 
     @pl.when(late)
     def late_part():
@@ -602,16 +596,18 @@
             remote(facts, place, send6, recv6.at[number - 1], served(number)).wait_recv()
             tables.append(list_tables(land_facts[number - 1, 0:2, 0, :]))
         wait_rows(land1, CHIPS - 1, recv1)
-        with_other_core(land1, land2, send2, recv2)
-
+        core_copy = remote(land1, land2, send2, recv2, other_core)
+        core_copy.start()
         kept = turn_received([land1[:, n, 0, :] for n in range(3)])
+        for number in range(SHARE):
+            halves[number] = pick(kept, core, core, number, *tables[number])
+        core_copy.wait()
+
         given = turn_received([land2[:, n, 0, :] for n in range(3)])
-        first = [jnp.where(core == 0, a, b) for a, b in zip(kept, given)]
-        second = [jnp.where(core == 0, b, a) for a, b in zip(kept, given)]
         tiles = range(2 * SHARE)
         entries, centres = [], []
         for number in range(SHARE):
-            found = pick(first, second, core, number, *tables[number])
+            found = halves[number] + pick(given, 1 - core, core, number, *tables[number])
             known = facts[2] if number == 0 else land_facts[number - 1, 2]
             for part in range(2):
                 chosen = found[:, 256 * part : 256 * part + 256]
@@ -829,6 +825,7 @@
             pltpu.VMEM((RENDER, 3, 1, 128), f32),
             pltpu.VMEM((CHIPS, 3, 1, 128), f32),
             pltpu.VMEM((CHIPS, 3, 1, 128), f32),
+            pltpu.VMEM((SHARE, 9, 512), f32),
             pltpu.VMEM((2 * CHIPS, 2, 128), f32),
             pltpu.VMEM((2 * RENDER, 2, 128), f32),
             pltpu.VMEM((3, 1, 256), f32),

time: 42 us -> 41.9 us (level)
  no operation moved by 1% of the time
where the time goes in v8:
time: 41.9 us; the launch traced here: 41.8 us
  Pallas kernels  41.1 us (98%)
  between operations  0.64 us (2%)
    pallas_call x1, Pallas kernels, body(): pl.pallas_call(exchange, out_shape=(jax.ShapeDtypeStruct((VIEWS, 40, 128)...  38.7 us
    pallas_call x1, Pallas kernels, body(): pl.pallas_call(update, out_shape=(whole, whole, whole, jax.ShapeDtypeStru...  2.39 us

profile of v8, /device:TPU:1, one launch (start us, length us, event | category | flops | bytes accessed | tf_op | source)
XLA Modules:
  0.0 41.8 jit_solution(17671076273322882004)
XLA Ops:
  0.6 38.7 %exchange.1 = (f32[4,40,128]{2,1,0:T(8,128)}, f32[1,128]{1,0:T(1,128)}) custom-call(f32[59,512]{1,0:T(8,128)} %params_in.3, f32[1,12]{1,0:T(1,128)} %camera_in.1, s32[1,1,512]{2,1,0:T(1,128)} %rows_in.1, s32[1,2,256]{2,1,0:T(2,128)} %lists_in.1, s32[1,2]{1,0:T(1,128)} %counts_in.1, s32[1,2]{1,0:T(1,128)} %tile_ids_in.1, f32[3,2,256]{2,1,0:T(2,128)} %bitcast.5), custom_call_target="tpu_custom_call" | custom-call | tf_op jit(solution)/shard_map/exchange/pallas_call | solution.py:809
  39.4 2.4 %update.1 = (f32[59,512]{1,0:T(8,128)}, f32[59,512]{1,0:T(8,128)}, f32[59,512]{1,0:T(8,128)}, f32[1,2]{1,0:T(1,128)}) custom-call(f32[59,512]{1,0:T(8,128)} %params_in.3, f32[59,512]{1,0:T(8,128)} %first_in.1, f32[59,512]{1,0:T(8,128)} %second_in.1, f32[160,128]{1,0:T(8,128)} %bitcast.4, f32[1,128]{1,0:T(1,128)} %get-tuple-element.7.loss_in), custom_call_target="tpu_custom_call" | custom-call | tf_op jit(solution)/shard_map/update/pallas_call | solution.py:873

commit v9 on v8

--- a/solution.py
+++ b/solution.py
@@ -208,7 +208,7 @@
     return rows
 
 
-def unpack_messages(messages, table):
+def unpack_messages(messages):
     turned = jnp.transpose(jnp.concatenate([messages, jnp.zeros_like(messages)], axis=0))
     keep = iota((16, 128), 1) < 64
     parts = []
@@ -216,7 +216,7 @@
         left = turned[32 * pair : 32 * pair + 16]
         right = turned[32 * pair + 16 : 32 * pair + 32]
         parts.append(jnp.where(keep, left, swap(right)))
-    return dot_rows_exact(jnp.concatenate(parts, axis=1), table)
+    return jnp.concatenate(parts, axis=1)
 
 
 def list_tables(lists):
@@ -701,29 +701,37 @@
         zero, one = land4[0:RENDER, pair, :], land4[RENDER:, pair, :]
         messages.append(jnp.where(low_rows, zero, swap(one)))
         messages.append(jnp.where(low_rows, swap(zero), one))
-    returned = unpack_messages(jnp.concatenate(messages, axis=0), table[...])
+    returned = unpack_messages(jnp.concatenate(messages, axis=0))
 
     lanes = iota((1, 128), 1)
     pose = jnp.zeros((1, 128), f32)
     for n in range(12):
         pose = jnp.where(lanes == n, scalars[n], pose)
-    for part in range(4):
-        own[10 * part : 10 * part + 9, :] = returned[0:9, 128 * part : 128 * part + 128]
-        own[10 * part + 9 : 10 * part + 10, :] = pose
-
-    def share(step, other, device):
-        remote(own, out.at[view], send5.at[step], recv5.at[view], device).start()
-
-    def take(step, other, device):
-        remote(own, out.at[other], send5.at[step], recv5.at[other], device).wait()
-
-    over_views(share)
+    def share(half, step, other, device):
+        rows_here = pl.ds(24 * half, 24)
+        place = out.at[view, rows_here]
+        sent, arrived = send5.at[half, step], recv5.at[half, view]
+        remote(own.at[rows_here], place, sent, arrived, device).start()
+
+    def take(half, step, other, device):
+        rows_here = pl.ds(24 * half, 24)
+        place = out.at[other, rows_here]
+        remote(own.at[rows_here], place, send5.at[half, step], recv5.at[half, other], device).wait()
+
+    for half in range(2):
+        ordered = dot_rows_exact(returned, table[256 * half : 256 * half + 256, :])
+        for part in range(2):
+            block = [ordered[0:9, 128 * part : 128 * part + 128], pose, jnp.zeros((2, 128), f32)]
+            start = 24 * half + 12 * part
+            own[start : start + 12, :] = jnp.concatenate(block, axis=0)
+        over_views(lambda *peer, half=half: share(half, *peer))
     keep = pltpu.make_async_copy(own, out.at[view], kept5)
     keep.start()
     pl.when(early)(lambda: wait_rows(back2, 2 * CHIPS - 1, send4))
     loss_copy.wait()
     keep.wait()
-    over_views(take)
+    for half in range(2):
+        over_views(lambda *peer, half=half: take(half, *peer))
 
 
 def update(
@@ -766,7 +774,7 @@
             spread[start : start + 59, :] = block
     columns = [spread[pl.ds(n, 16, stride=64), :] for n in range(59)]
     copies[1].wait()
-    given = [grads[pl.ds(n, 16, stride=10), :] for n in range(10)]
+    given = [grads[pl.ds(n, 16, stride=12), :] for n in range(10)]
     camera = [given[9][:, n : n + 1] for n in range(12)]
 
     def shown(rows):
@@ -809,7 +817,7 @@
     grads, loss = pl.pallas_call(
         exchange,
         out_shape=(
-            jax.ShapeDtypeStruct((VIEWS, 40, 128), f32),
+            jax.ShapeDtypeStruct((VIEWS, 48, 128), f32),
             jax.ShapeDtypeStruct((1, 128), f32),
         ),
         in_specs=[hbm] * 7,
@@ -832,7 +840,7 @@
             pltpu.VMEM((SHARE - 1, 3, 1, 256), f32),
             pltpu.VMEM((6, 1, 256), f32),
             pltpu.VMEM((SHARE - 1, 6, 1, 256), f32),
-            pltpu.VMEM((40, 128), f32),
+            pltpu.VMEM((48, 128), f32),
             pltpu.VMEM((1, 128), f32),
             pltpu.VMEM((SHARE - 1, 1, 128), f32),
             pltpu.VMEM((2 * SHARE, 256, 256), f32),
@@ -846,8 +854,8 @@
             dma,
             dma,
             dma,
-            dma((VIEWS,)),
-            dma((VIEWS,)),
+            dma((2, VIEWS)),
+            dma((2, VIEWS)),
             dma,
             dma,
             dma((SHARE - 1,)),
@@ -879,7 +887,7 @@
             near,
             near,
             near,
-            pltpu.VMEM((VIEWS * 40, 128), f32),
+            pltpu.VMEM((VIEWS * 48, 128), f32),
             pltpu.VMEM((1, 128), f32),
             pltpu.VMEM((1024, 128), f32),
             pltpu.VMEM((256, 128), f32),
@@ -887,7 +895,7 @@
         ],
         compiler_params=some,
         name="update",
-    )(params, first_moment, second_moment, grads.reshape(VIEWS * 40, 128), loss)
+    )(params, first_moment, second_moment, grads.reshape(VIEWS * 48, 128), loss)
 
 
 def solution(mesh):

time: 41.9 us -> 42.1 us (level)
  no operation moved by 1% of the time
where the time goes in v9:
time: 42.1 us; the launch traced here: 41.9 us
  Pallas kernels  41.3 us (98%)
  between operations  0.64 us (2%)
    pallas_call x1, Pallas kernels, body(): pl.pallas_call(exchange, out_shape=(jax.ShapeDtypeStruct((VIEWS, 48, 128)...  38.9 us
    pallas_call x1, Pallas kernels, body(): pl.pallas_call(update, out_shape=(whole, whole, whole, jax.ShapeDtypeStru...  2.39 us

profile of v9, /device:TPU:1, one launch (start us, length us, event | category | flops | bytes accessed | tf_op | source)
XLA Modules:
  0.0 41.9 jit_solution(3492796222801914977)
XLA Ops:
  0.6 38.9 %exchange.1 = (f32[4,48,128]{2,1,0:T(8,128)}, f32[1,128]{1,0:T(1,128)}) custom-call(f32[59,512]{1,0:T(8,128)} %params_in.3, f32[1,12]{1,0:T(1,128)} %camera_in.1, s32[1,1,512]{2,1,0:T(1,128)} %rows_in.1, s32[1,2,256]{2,1,0:T(2,128)} %lists_in.1, s32[1,2]{1,0:T(1,128)} %counts_in.1, s32[1,2]{1,0:T(1,128)} %tile_ids_in.1, f32[3,2,256]{2,1,0:T(2,128)} %bitcast.5), custom_call_target="tpu_custom_call" | custom-call | tf_op jit(solution)/shard_map/exchange/pallas_call | solution.py:817
  39.5 2.4 %update.1 = (f32[59,512]{1,0:T(8,128)}, f32[59,512]{1,0:T(8,128)}, f32[59,512]{1,0:T(8,128)}, f32[1,2]{1,0:T(1,128)}) custom-call(f32[59,512]{1,0:T(8,128)} %params_in.3, f32[59,512]{1,0:T(8,128)} %first_in.1, f32[59,512]{1,0:T(8,128)} %second_in.1, f32[192,128]{1,0:T(8,128)} %bitcast.4, f32[1,128]{1,0:T(1,128)} %get-tuple-element.7.loss_in), custom_call_target="tpu_custom_call" | custom-call | tf_op jit(solution)/shard_map/update/pallas_call | solution.py:881
